TPU v7x, 256 devices: a whole 4x4x8 slice. The times are simulated.
256 devices in a mesh: gx: 16 (over z, core), gy: 16 (over y, x).
Axes of the slice: x: 4, y: 4, z: 8, core: 2. Of those that a mesh axis runs over, the one named last changes fastest.
Arguments:
- rhs: float32 [128, 128, 6, 3, 256], P('gx', 'gy'), may hold values from -400 to 400
- contrast: float32 [128, 128, 256], P('gx', 'gy'), may hold values from 0.2 to 2
- occupied: int32 [128, 128], P('gx', 'gy'), may hold values 0 or 1
- near: bfloat16 [5, 768, 768], replicated, may hold values from -0.078125 to 0.078125
- basis: bfloat16 [768, 64], replicated, may hold values from -0.21875 to 0.21875
- transfer: float32 [5, 4, 64, 64], replicated, may hold values from -0.5 to 0.5
- coupling: float32 [6, 20, 64, 64], replicated, may hold values from -0.15625 to 0.15625
Outputs:
- third: float32 [128, 128, 6, 3, 256], P('gx', 'gy')
- hess: float32 [6, 6], replicated
All inputs are finite; a program needn't handle non-finite values. No bound on the sum of `occupied` on one device may be relied on, other than what follows from the above.
Results may differ from a plain program's by a relative error of at most 0.0031.
Values may be sent and summed in bfloat16 or wider, within the bound.
No kernel may reach another device: no remote copies, remote signals or barrier semaphores. Data moves between devices by JAX's collectives and lax.ppermute only.
A program may use at most 128 MiB of HBM per device.

v0:
```python
import functools

import jax
import jax.numpy as jnp
from jax import lax
from jax.experimental import pallas as pl
from jax.experimental.pallas import tpu as pltpu
from jax.sharding import Mesh
from jax.sharding import PartitionSpec as P

F32, BF16 = jnp.float32, jnp.bfloat16
GX = ("z", "c")
GY = ("y", "x1", "x0")
CLASS_ORDER = ("c", "x0", "z", "y", "x1")
EVERYONE = ("z", "c", "y", "x1", "x0")
EPSILON = 1e-06
EXACT = lax.Precision.HIGHEST
HALF = ((1, -1), (1, 0), (1, 1), (0, 1))
AROUND = HALF + tuple((-a, -b) for a, b in HALF)
NEAR_SLOT = {(0, 0): 0, (1, -1): 1, (1, 0): 2, (1, 1): 3, (0, 1): 4}
FAR = [
    (dx, dy)
    for dx in range(-3, 4)
    for dy in range(-3, 4)
    if max(abs(dx), abs(dy)) >= 2 and (dx > 0 or (dx == 0 and dy > 0))
]
VMEM = pl.BlockSpec(memory_space=pltpu.VMEM)
SMEM = pl.BlockSpec(memory_space=pltpu.SMEM)
CHILDREN = [(c, e) for c in range(2) for e in range(2)]
PARENTS = (4, 2, 1)


def dot(a, b):
    return jnp.dot(a, b, preferred_element_type=F32)


def dot_t(a, b, precision=None):
    return lax.dot_general(
        a, b, (((1,), (1,)), ((), ())), preferred_element_type=F32, precision=precision
    )


def call(kernel, outs, specs, scratch, flops, *args):
    moved = sum(a.size * a.dtype.itemsize for a in args)
    return pl.pallas_call(
        kernel,
        out_shape=outs,
        in_specs=specs,
        out_specs=jax.tree.map(lambda _: VMEM, outs),
        scratch_shapes=scratch,
        compiler_params=pltpu.CompilerParams(vmem_limit_bytes=50 * 2**20),
        cost_estimate=pl.CostEstimate(flops=flops, bytes_accessed=moved, transcendentals=0),
    )(*args)


def pair_blocks(coupling_ref, inner_ref, high_ref, low_ref):
    zero = jnp.zeros((64, 64), F32)
    for level in range(6):
        flipped = {}
        for n, (dp, dq) in enumerate(HALF):
            for c_in, e_in in CHILDREN:
                for c in range(2):
                    row = []
                    for e in range(2):
                        d = (2 * dp + c_in - c, 2 * dq + e_in - e)
                        if max(abs(d[0]), abs(d[1])) < 2:
                            row.append(zero)
                        elif d in FAR:
                            row.append(coupling_ref[level, FAR.index(d)])
                        else:
                            k = FAR.index((-d[0], -d[1]))
                            if k not in flipped:
                                flipped[k] = coupling_ref[level, k].T
                            row.append(flipped[k])
                    r0 = (2 * c_in + e_in) * 64
                    rows, lanes = slice(r0, r0 + 64), slice(c * 128, c * 128 + 128)
                    block = jnp.concatenate(row, axis=1)
                    high = block.astype(BF16)
                    if level < 3:
                        inner_ref[level, n, rows, lanes] = high
                    else:
                        high_ref[level - 3, n, rows, lanes] = high
                        low_ref[level - 3, n, rows, lanes] = (block - high.astype(F32)).astype(BF16)


def in_two(x):
    high = x.astype(BF16)
    return high, (x - high.astype(F32)).astype(BF16)


def couple(x, pairs, level, k):
    high, low = in_two(x)
    product = dot if k < 4 else dot_t
    both = product(jnp.concatenate([high, low], axis=0), pairs[0][level, k % 4])
    out = both[0 : x.shape[0]] + both[x.shape[0] :]
    if len(pairs) > 1:
        out = out + product(high, pairs[1][level, k % 4])
    return out


def weight_rows(contrast_ref, occupied_ref, i):
    square = (8, 8)
    here = jnp.broadcast_to(occupied_ref[i : i + 1, :].astype(F32), square)
    same = lax.broadcasted_iota(jnp.int32, square, 0) == lax.broadcasted_iota(jnp.int32, square, 1)
    occupied = jnp.sum(jnp.where(same, here, 0.0), axis=1, keepdims=True)
    w = occupied * contrast_ref[8 * i : 8 * i + 8, :]
    return jnp.concatenate([jnp.concatenate([w] * 6, axis=0)] * 3, axis=1)


def lanes_to_one(x):
    total = x[:, 0:128]
    for k in range(1, x.shape[1] // 128):
        total = total + x[:, 128 * k : 128 * k + 128]
    return total


def field_row(sums):
    lane = lax.broadcasted_iota(jnp.int32, (1, 128), 1)
    row = jnp.zeros((1, 128), F32)
    for n, acc in enumerate(sums):
        for f in range(6):
            row = row + jnp.where(lane == 6 * n + f, jnp.sum(acc[8 * f : 8 * f + 8, :]), 0.0)
    return row


def left_half(shape):
    return lax.broadcasted_iota(jnp.int32, shape, len(shape) - 1) < 64


def tiles(ref, rows):
    return jnp.concatenate([ref[t, rows, :] for t in range(ref.shape[0])], axis=1)


def spread_skeleton(field_at, sums_row, refs, skel):
    contrast_ref, occupied_ref, basis_ref, transfer_ref = refs[0]
    src_ref, up_ref, down_ref, pay_ref, *tree = refs[1]
    twice = jnp.concatenate([basis_ref[...]] * 2, axis=0)
    for i in range(8):
        rows = slice(48 * i, 48 * i + 48)
        s = (weight_rows(contrast_ref, occupied_ref, i) * field_at(i)).astype(BF16)
        for t in range(6):
            src_ref[t, rows, :] = s[:, 128 * t : 128 * t + 128].astype(F32)
        skel[rows, :] = dot_t(s, twice)
        if i == 0:
            down_ref[:, 0:768] = s
        if i == 7:
            up_ref[:, 0:768] = s
    half = left_half((6, 128))
    for level, n in enumerate(PARENTS):
        node = tree[level]
        node[...] = jnp.zeros(node.shape, F32)
        offset = min(level, 1)
        for i in range(2 * n):
            for q in range(n):
                at = 48 * i + offset + 2 * q
                node[i % 2, pl.ds((i // 2 + 1) * 48 + 1 + q, 6, stride=8), :] = jnp.where(
                    half, skel[pl.ds(at, 6, stride=8), :], skel[pl.ds(at + 1, 6, stride=8), :]
                )
        lanes = slice(768 + 256 * level, 1024 + 256 * level)
        up_ref[:, lanes] = tiles(node, slice(48 * n, 48 * n + 48)).astype(BF16)
        down_ref[:, lanes] = tiles(node, slice(48, 96)).astype(BF16)
        skel[0 : 48 * n, :] = jnp.dot(
            tiles(node, slice(48, 48 * n + 48)),
            transfer_ref[level],
            precision=EXACT,
            preferred_element_type=F32,
        )
    top = skel[pl.ds(1, 6, stride=8), :]
    pay = jnp.concatenate([jnp.where(half[0:3], top[0:3, :], top[3:6, :]), sums_row], axis=0)
    pay_ref[...] = jnp.broadcast_to(pay[None], pay_ref.shape)


SOURCE_OUTS = [
    jax.ShapeDtypeStruct((6, 384, 128), F32),
    jax.ShapeDtypeStruct((48, 1536), BF16),
    jax.ShapeDtypeStruct((48, 1536), BF16),
    jax.ShapeDtypeStruct((256, 4, 128), F32),
    jax.ShapeDtypeStruct((2, 288, 128), F32),
    jax.ShapeDtypeStruct((2, 192, 128), F32),
    jax.ShapeDtypeStruct((2, 144, 128), F32),
]
SOURCE_SCRATCH = [pltpu.VMEM((384, 128), F32)]


def first_source(x_ref, contrast_ref, occupied_ref, basis_ref, transfer_ref, *rest):
    outs, skel = rest[:7], rest[7]
    acc = jnp.zeros((48, 128), F32)
    for i in range(8):
        x = x_ref[48 * i : 48 * i + 48, :]
        acc = acc + lanes_to_one(x * x)
    spread_skeleton(
        lambda i: x_ref[48 * i : 48 * i + 48, :],
        field_row([acc]),
        ((contrast_ref, occupied_ref, basis_ref, transfer_ref), outs),
        skel,
    )


def columns(pos_ref, src_ref, a0, a1, a2, above_ref, below_ref, left_ref, right_ref, above, below):
    gx = pos_ref[0]
    for t in range(12):
        lanes = slice(128 * t, 128 * t + 128)
        above[t] = above_ref[:, lanes].astype(F32) * (gx > 0).astype(F32)
        below[t] = below_ref[:, lanes].astype(F32) * (gx < 15).astype(F32)
    for out, side in ((left_ref, 0), (right_ref, 1)):
        j = 7 * side
        for t in range(6):
            out[0:60, 128 * t : 128 * t + 128] = jnp.concatenate(
                [
                    above[t, pl.ds(j, 6, stride=8), :],
                    src_ref[t, pl.ds(j, 48, stride=8), :],
                    below[t, pl.ds(j, 6, stride=8), :],
                ],
                axis=0,
            ).astype(BF16)
            out[60:80, 128 * t : 128 * t + 128] = jnp.zeros((20, 128), BF16)
        for t in range(2):
            parts = []
            for level, (node, n) in enumerate(zip((a0, a1, a2), PARENTS)):
                q = n if side else 1
                parts += [
                    above[6 + 2 * level + t, pl.ds(q, 6, stride=8), :],
                    node[t, pl.ds(48 + q, 6 * n, stride=8), :],
                    below[6 + 2 * level + t, pl.ds(q, 6, stride=8), :],
                ]
            parts.append(jnp.zeros((2, 128), F32))
            out[:, 768 + 128 * t : 896 + 128 * t] = jnp.concatenate(parts, axis=0).astype(BF16)


def near_and_low(
    pos_ref, src_ref, a0, a1, a2, above_ref, below_ref, left_ref, right_ref, near_ref, inner_ref,
    near_out, o0, o1, o2, wide, moved, edge, placed, n0, n1, n2, turned,
):
    gx, gy = pos_ref[0], pos_ref[1]
    up = (gx > 0).astype(F32)
    down = (gx < 15).astype(F32)
    for t in range(6):
        lanes = slice(128 * t, 128 * t + 128)
        wide[t, 0:48, :] = above_ref[:, lanes].astype(F32) * up
        wide[t, 48:432, :] = src_ref[t]
        wide[t, 432:480, :] = below_ref[:, lanes].astype(F32) * down
    flags = ((gy > 0).astype(F32), (gy < 15).astype(F32))
    first = True
    for b in (0, -1, 1):
        side_ref, flag = ((left_ref, flags[0]), (right_ref, flags[1]))[b > 0]
        if b != 0:
            edge[...] = side_ref[:, 0:768].astype(F32) * flag
        for t in range(6):
            lanes = slice(128 * t, 128 * t + 128)
            if b == 0:
                placed[:, lanes] = wide[t].astype(BF16)
                continue
            if b < 0:
                moved[t, 1:480, :] = wide[t, 0:479, :]
                moved[t, pl.ds(0, 60, stride=8), :] = edge[0:60, lanes]
            else:
                moved[t, 0:479, :] = wide[t, 1:480, :]
                moved[t, pl.ds(7, 60, stride=8), :] = edge[0:60, lanes]
            placed[:, lanes] = moved[t].astype(BF16)
        for a in (-1, 0, 1):
            lhs = placed[48 * (1 + a) : 48 * (1 + a) + 384, :]
            if (a, b) in NEAR_SLOT:
                part = dot(lhs, near_ref[NEAR_SLOT[a, b]])
            else:
                part = dot_t(lhs, near_ref[NEAR_SLOT[-a, -b]])
            if first:
                near_out[...] = part
                first = False
            else:
                near_out[...] += part
    start = 0
    for level, (node, full, out, n) in enumerate(
        zip((a0, a1, a2), (n0, n1, n2), (o0, o1, o2), PARENTS)
    ):
        size, lanes = 48 * (n + 2), slice(768 + 256 * level, 1024 + 256 * level)
        for t in range(2):
            lane = slice(lanes.start + 128 * t, lanes.start + 128 * t + 128)
            full[t] = node[t]
            full[t, 0:48, :] = above_ref[:, lane].astype(F32) * up
            full[t, size - 48 : size, :] = below_ref[:, lane].astype(F32) * down
        for side_ref, flag, q in ((left_ref, flags[0], 0), (right_ref, flags[1], n + 1)):
            edge[:, 0:256] = side_ref[:, 768:1024].astype(F32) * flag
            for t in range(2):
                full[t, pl.ds(q, 6 * (n + 2), stride=8), :] = edge[
                    start : start + 6 * (n + 2), 128 * t : 128 * t + 128
                ]
        total = jnp.zeros((48 * n, 256), F32)
        for dq in (-1, 0, 1):
            for t in range(2):
                lane = slice(128 * t, 128 * t + 128)
                if dq == 0:
                    turned[0:size, lane] = full[t]
                elif dq < 0:
                    turned[1:size, lane] = full[t, 0 : size - 1, :]
                    turned[0:1, lane] = full[t, 0:1, :]
                else:
                    turned[0 : size - 1, lane] = full[t, 1:size, :]
                    turned[size - 1 : size, lane] = full[t, 0:1, :]
            for k, (dp, dq_k) in enumerate(AROUND):
                if dq_k == dq:
                    lhs = turned[48 * (1 + dp) : 48 * (1 + dp) + 48 * n, :]
                    total = total + couple(lhs, (inner_ref,), level, k)
        out[...] = total
        start += 6 * (n + 2)


def lane_of(f):
    return (f % 3) * 128 + (f // 3) * 64


def select(chosen, table):
    high, low = in_two(table)
    return dot(chosen, high) + dot(chosen, low)


def far_above(pos_ref, all_ref, pairs, transfer_ref, by_child, grown, side_by):
    gx, gy = pos_ref[0], pos_ref[1]
    table = jnp.concatenate([all_ref[pl.ds(m, 256, stride=4), :] for m in range(3)], axis=1)
    classes = table
    row = lax.broadcasted_iota(jnp.int32, (32, 1), 0)
    around, child = row % 8, row // 8
    shift_p = sum(jnp.where(around == k, dp, 0) for k, (dp, _) in enumerate(AROUND))
    shift_q = sum(jnp.where(around == k, dq, 0) for k, (_, dq) in enumerate(AROUND))
    outs = []
    for step in range(3):
        n = 16 >> step
        at_p, at_q = (gx >> (step + 1)) + shift_p, (gy >> (step + 1)) + shift_q
        inside = (at_p >= 0) & (at_p < n // 2) & (at_q >= 0) & (at_q < n // 2)
        if step == 0:
            where = child * (n * n // 4) + at_p * (n // 2) + at_q
        else:
            where = (2 * at_p + child // 2) * n + 2 * at_q + child % 2
        lane = lax.broadcasted_iota(jnp.int32, (32, n * n), 1)
        chosen = ((lane == where) & inside).astype(F32).astype(BF16)
        picked = select(chosen, table)
        by_child[...] = jnp.zeros(by_child.shape, F32)
        for f in range(6):
            for k in range(4):
                by_child[k // 2, 8 * f : 8 * f + 8, 64 * (k % 2) : 64 * (k % 2) + 64] = picked[
                    8 * k : 8 * k + 8, lane_of(f) : lane_of(f) + 64
                ]
        total = jnp.zeros((8, 256), F32)
        for k in range(8):
            lhs = tiles(by_child, pl.ds(k, 8, stride=8))
            total = total + couple(lhs, pairs, step, k)
        outs.append(total)
        if step == 2:
            break
        m = n * n // 4
        if step == 1:
            r = lax.broadcasted_iota(jnp.int32, (n * n, 1), 0)
            k, p, q = r // m, (r % m) // (n // 2), r % (n // 2)
            from_row = (2 * p + k // 2) * n + 2 * q + k % 2
            lane = lax.broadcasted_iota(jnp.int32, (n * n, n * n), 1)
            classes = select((lane == from_row).astype(F32).astype(BF16), table)
        for f in range(6):
            for k in range(4):
                side_by[m * f : m * f + m, 64 * k : 64 * k + 64] = classes[
                    m * k : m * k + m, lane_of(f) : lane_of(f) + 64
                ]
        lifted = jnp.dot(
            side_by[0 : 6 * m, :],
            transfer_ref[3 + step, :, 0:64],
            precision=EXACT,
            preferred_element_type=F32,
        )
        for f in range(6):
            grown[0:m, lane_of(f) : lane_of(f) + 64] = lifted[m * f : m * f + m, :]
        table = grown[0:m, :]

    def own_child(x, step):
        bit_x, bit_y = (gx >> step) & 1, (gy >> step) & 1
        rows = [x[:, 64 * k : 64 * k + 64] for k in range(4)]
        low = jnp.where(bit_y == 1, rows[1], rows[0])
        high = jnp.where(bit_y == 1, rows[3], rows[2])
        return jnp.where(bit_x == 1, high, low)

    reached = own_child(outs[2], 2)
    for step in (1, 0):
        reached = own_child(outs[step] + dot_t(reached, transfer_ref[3 + step, :, 0:64], EXACT), step)
    return jnp.concatenate([reached, jnp.zeros((8, 64), F32)], axis=1)


def far_down(reached, o0, o1, o2, transfer_ref, flat, held):
    half = left_half((6, 128))
    flat[...] = jnp.zeros(flat.shape, F32)
    flat[pl.ds(1, 8, stride=8), :] = reached
    for level, out in ((2, o2), (1, o1), (0, o0)):
        n = PARENTS[level]
        value = out[...] + dot_t(flat[0 : 48 * n, :], transfer_ref[level], EXACT)
        for t in range(2):
            held[t, 0 : 48 * n, :] = value[:, 128 * t : 128 * t + 128]
        offset = min(level, 1)
        for i in range(2 * n):
            for q in range(n):
                both = held[i % 2, pl.ds((i // 2) * 48 + 1 + q, 6, stride=8), :]
                at = 48 * i + offset + 2 * q
                flat[pl.ds(at, 6, stride=8), :] = jnp.where(half, both, 0.0)
                flat[pl.ds(at + 1, 6, stride=8), :] = jnp.where(half, 0.0, both)


def image_rows(i, flat, basis_ref, near_ref):
    d = flat[48 * i : 48 * i + 48, :]
    high = d.astype(BF16)
    low = (d - high.astype(F32)).astype(BF16)
    basis = jnp.concatenate([basis_ref[...]] * 4, axis=0)
    far = dot(jnp.concatenate([high, low], axis=1), basis)
    return near_ref[48 * i : 48 * i + 48, :] + far


def per_row(totals, slot):
    lane = lax.broadcasted_iota(jnp.int32, (1, 128), 1)
    field = lax.broadcasted_iota(jnp.int32, (48, 1), 0) // 8
    out = jnp.zeros((48, 1), F32)
    for f in range(6):
        out = out + jnp.where(
            field == f, jnp.sum(jnp.where(lane == 6 * slot + f, totals, 0.0)), 0.0
        )
    return out


FAR_SCRATCH = [
    pltpu.VMEM((2, 64, 128), F32),
    pltpu.VMEM((64, 384), F32),
    pltpu.VMEM((384, 256), F32),
    pltpu.VMEM((384, 128), F32),
    pltpu.VMEM((2, 192, 128), F32),
]


def second_source(
    pos_ref, all_ref, x_ref, near_ref, o0, o1, o2, high_ref, low_ref, contrast_ref, occupied_ref, basis_ref,
    transfer_ref, u_ref, *rest,
):
    outs, (by_child, grown, side_by, flat, held, skel) = rest[:7], rest[7:]
    reached = far_above(pos_ref, all_ref, (high_ref, low_ref), transfer_ref, by_child, grown, side_by)
    far_down(reached, o0, o1, o2, transfer_ref, flat, held)
    cross = jnp.zeros((48, 128), F32)
    square = jnp.zeros((48, 128), F32)
    for i in range(8):
        u = image_rows(i, flat, basis_ref, near_ref)
        u_ref[48 * i : 48 * i + 48, :] = u
        cross = cross + lanes_to_one(u * x_ref[48 * i : 48 * i + 48, :])
        square = square + lanes_to_one(u * u)
    spread_skeleton(
        lambda i: u_ref[48 * i : 48 * i + 48, :],
        field_row([cross, square]),
        ((contrast_ref, occupied_ref, basis_ref, transfer_ref), outs),
        skel,
    )


def scales(first_totals, second_totals, count):
    s = per_row(first_totals, 0) / count
    beta = jnp.sqrt(s + EPSILON)
    off_one = EPSILON / (s + EPSILON)
    one = s / (s + EPSILON)
    p = per_row(second_totals, 0) / count / (s + EPSILON)
    q = per_row(second_totals, 1) / count / (s + EPSILON)
    r = q + (off_one - p) * ((off_one - p) * one + 2.0 * p)
    h21 = jnp.sqrt(r + EPSILON)
    h11 = one + p
    return dict(
        beta=beta, h11=h11, h21=h21, lean=off_one - p, one=one,
        f12=off_one * h11 / h21, n2=r / (r + EPSILON), off_two=EPSILON / (r + EPSILON),
    )


def totals_of(all_ref):
    return jnp.sum(all_ref[pl.ds(3, 256, stride=4), :], axis=0, keepdims=True)


def last_sums(
    count, pos_ref, all_ref, before_ref, x_ref, u_ref, near_ref, o0, o1, o2, high_ref, low_ref, basis_ref,
    transfer_ref, v_ref, sums_ref, totals_ref, by_child, grown, side_by, flat, held,
):
    first_totals, second_totals = totals_of(before_ref), totals_of(all_ref)
    totals_ref[0:1, :] = first_totals
    totals_ref[1:2, :] = second_totals
    k = scales(first_totals, second_totals, count)
    over, over_two = 1.0 / k["beta"], 1.0 / k["h21"]
    reached = far_above(pos_ref, all_ref, (high_ref, low_ref), transfer_ref, by_child, grown, side_by)
    far_down(reached, o0, o1, o2, transfer_ref, flat, held)
    sums = [jnp.zeros((48, 128), F32)] * 3
    for i in range(8):
        rows = slice(48 * i, 48 * i + 48)
        first = x_ref[rows, :] * over
        image = u_ref[rows, :] * over
        second = (k["lean"] * first + image) * over_two
        v = (k["lean"] * image + image_rows(i, flat, basis_ref, near_ref) * over) * over_two
        v_ref[rows, :] = v
        sums = [
            s + lanes_to_one(w * v) for s, w in zip(sums, (first, second, v))
        ]
    lane = lax.broadcasted_iota(jnp.int32, (1, 128), 1)
    row = jnp.zeros((1, 128), F32)
    for n, acc in enumerate(sums):
        for f in range(6):
            row = row + jnp.where(lane == 16 * n + f, jnp.sum(acc[8 * f : 8 * f + 8, :]), 0.0)
    sums_ref[...] = jnp.broadcast_to(row[None], sums_ref.shape)


def finish(count, sums_ref, totals_ref, x_ref, u_ref, v_ref, third_ref, hess_ref, table):
    k = scales(totals_ref[0:1, :], totals_ref[1:2, :], count)
    total = jnp.sum(sums_ref[...], axis=0, keepdims=True) / count
    lane = lax.broadcasted_iota(jnp.int32, (1, 128), 1)
    field = lax.broadcasted_iota(jnp.int32, (48, 1), 0) // 8

    def rows_of(n):
        out = jnp.zeros((48, 1), F32)
        for f in range(6):
            out = out + jnp.where(
                field == f, jnp.sum(jnp.where(lane == 16 * n + f, total, 0.0)), 0.0
            )
        return out

    c1, c2, t = rows_of(0), rows_of(1), rows_of(2)
    h12, h22 = k["f12"] + c1, k["n2"] + c2
    g = k["off_two"] - c2
    rest = (
        t + g * g * k["n2"] + h12 * h12 * k["one"] + 2.0 * g * c2
        - 2.0 * h12 * c1 - 2.0 * g * h12 * k["f12"]
    )
    h32 = jnp.sqrt(rest + EPSILON)
    over, over_two, over_three = 1.0 / k["beta"], 1.0 / k["h21"], 1.0 / h32
    for i in range(8):
        rows = slice(48 * i, 48 * i + 48)
        first = x_ref[rows, :] * over
        second = (k["lean"] * first + u_ref[rows, :] * over) * over_two
        third_ref[rows, :] = (v_ref[rows, :] + g * second - h12 * first) * over_three
    lane48 = lax.broadcasted_iota(jnp.int32, (48, 128), 1)
    out = jnp.zeros((48, 128), F32)
    for n, h in enumerate((k["beta"], k["h11"], k["h21"], h12, h22, h32)):
        out = out + jnp.where(lane48 == n, h, 0.0)
    table[...] = out
    hess_ref[...] = table[pl.ds(0, 6, stride=8), :][:, 0:6]


def turn(n, s):
    return [(i, (i + s) % n) for i in range(n)]


def to_everyone(blocks):
    return lax.all_to_all(blocks, CLASS_ORDER, 0, 0, tiled=True)


def body(rhs, contrast, occupied, near, basis, transfer, coupling):
    side, _, fields, comps, voxels = rhs.shape
    count = float(128 * 128 * comps * voxels)
    x = rhs.transpose(0, 2, 1, 3, 4).reshape(384, 768)
    contrast = contrast.reshape(64, voxels)
    stacked = transfer.reshape(5, 256, 64)
    stacked = jnp.concatenate([stacked] * 2, axis=2)
    basis = basis.T
    pos = jnp.stack([lax.axis_index(GX), lax.axis_index(GY)]).astype(jnp.int32)
    shape = jax.ShapeDtypeStruct
    inner, *outer = call(
        pair_blocks, [shape((3, 4, 256, 256), BF16)] * 3, [VMEM], [], 10**8, coupling
    )

    def exchange(outs, inner):
        src, up, down, pay, a0, a1, a2 = outs
        src, inner = lax.optimization_barrier((src, inner))
        above = lax.ppermute(up, GX, turn(16, 1))
        below = lax.ppermute(down, GX, turn(16, -1))
        to_left, to_right = call(
            columns, [shape((80, 1024), BF16)] * 2, [SMEM] + [VMEM] * 6,
            [pltpu.VMEM((12, 48, 128), F32)] * 2, 10**6,
            pos, src, a0, a1, a2, above, below,
        )
        pay, to_left, to_right = lax.optimization_barrier((pay, to_left, to_right))
        right = lax.ppermute(to_left, GY, turn(16, -1))
        left = lax.ppermute(to_right, GY, turn(16, 1))
        everyone = to_everyone(pay).reshape(1024, 128)
        parts = call(
            near_and_low,
            [shape((384, 768), F32), shape((192, 256), F32), shape((96, 256), F32), shape((48, 256), F32)],
            [SMEM] + [VMEM] * 10,
            [
                pltpu.VMEM((6, 480, 128), F32), pltpu.VMEM((6, 480, 128), F32), pltpu.VMEM((80, 768), F32),
                pltpu.VMEM((480, 768), BF16), pltpu.VMEM((2, 288, 128), F32), pltpu.VMEM((2, 192, 128), F32),
                pltpu.VMEM((2, 144, 128), F32), pltpu.VMEM((288, 256), F32),
            ],
            10**10,
            pos, src, a0, a1, a2, above, below, left, right, near, inner,
        )
        return everyone, parts

    outs = call(
        first_source, SOURCE_OUTS, [VMEM] * 5, SOURCE_SCRATCH, 10**8,
        x, contrast, occupied, basis, stacked,
    )
    all_one, parts = exchange(outs, inner)
    u, *outs = call(
        second_source, [shape((384, 768), F32)] + SOURCE_OUTS, [SMEM] + [VMEM] * 12,
        FAR_SCRATCH + SOURCE_SCRATCH, 10**8,
        pos, all_one, x, *parts, *outer, contrast, occupied, basis, stacked,
    )
    all_two, parts = exchange(outs, inner)
    v, sums, totals = call(
        functools.partial(last_sums, count),
        [shape((384, 768), F32), shape((256, 1, 128), F32), shape((8, 128), F32)],
        [SMEM] + [VMEM] * 12, FAR_SCRATCH, 10**8,
        pos, all_two, all_one, x, u, *parts, *outer, basis, stacked,
    )
    third, hess = call(
        functools.partial(finish, count),
        [shape((384, 768), F32), shape((6, 6), F32)], [VMEM] * 5, [pltpu.VMEM((48, 128), F32)], 10**6,
        to_everyone(sums).reshape(256, 128), totals, x, u, v,
    )
    third = third.reshape(side, fields, side, comps, voxels).transpose(0, 2, 1, 3, 4)
    return third, hess


def solution(mesh):
    grid = Mesh(mesh.devices.reshape(8, 2, 4, 2, 2), EVERYONE)
    placed = (P(GX, GY, None, None, None), P(GX, GY, None), P(GX, GY), P(), P(), P(), P())
    return jax.shard_map(
        body, mesh=grid, in_specs=placed,
        out_specs=(P(GX, GY, None, None, None), P()), check_vma=False,
    )
```

profile of v0, /device:TPU:1, one launch (start us, length us, event | category | flops | bytes accessed | tf_op | source)
XLA Modules:
  0.0 142.7 jit_solution(18268874816173746490)
XLA Ops:
  0.7 1.7 %pad_maximum_fusion.transfer_ref = f32[5,256,128]{2,1,0:T(8,128)S(1)} fusion(f32[5,256,64]{2,1,0:T(8,128)} %bitcast.27), kind=kLoop, calls=%fused_computation | loop fusion | flops 163840 | bytes 983040 | tf_op jit(solution)/shard_map/concatenate | solution.py:553
  2.4 3.9 %shard_map.86 = (f32[6,384,128]{2,1,0:T(8,128)S(1)}, bf16[48,1536]{1,0:T(8,128)(2,1)S(1)}, bf16[48,1536]{1,0:T(8,128)(2,1)S(1)}, f32[256,4,128]{2,1,0:T(4,128)},...) custom-call(f32[384,768]{1,0:T(8,128)} %bitcast.14, f32[64,256]{1,0:T(8,128)S(1)} %bitcast.25, ...), custom_call_target="tpu_custom_call" | custom-call | flops 100000000 | bytes 1999104 | tf_op jit(solution)/shard_map/pallas_call | solution.py:45
  6.3 3.0 %collective-permute-start = (bf16[48,1536]{1,0:T(8,128)(2,1)S(1)}, bf16[48,1536]{1,0:T(8,128)(2,1)S(1)}, u32[]{:S(2)}, u32[]{:S(2)}) collective-permute-start(bf16[48,1536]{1,0:T(8,128)(2,1)S(1)} %get-tuple-element.54), channel_id=1, source_target_pairs={{0,16},{16,32},{32,48},{48,64},{64,80},{80,96},{96,112},{112,128},... | collective-permute-start | bytes 442376 | tf_op jit(solution)/shard_map/ppermute | solution.py:564
  9.5 4.5 %shard_map.87 = (bf16[3,4,256,256]{3,2,1,0:T(8,128)(2,1)S(1)}, bf16[3,4,256,256]{3,2,1,0:T(8,128)(2,1)S(1)}, bf16[3,4,256,256]{3,2,1,0:T(8,128)(2,1)}) custom-call(f32[6,20,64,64]{3,2,1,0:T(8,128)} %coupling_ref.1), custom_call_target="tpu_custom_call" | custom-call | flops 100000000 | bytes 1966080 | tf_op jit(solution)/shard_map/pallas_call | solution.py:45
  14.0 1.2 copy-done.1
  15.2 1.1 copy-done.24
  16.4 1.4 shard_map.88
  18.8 3.8 %collective-permute-start.3 = (bf16[80,1024]{1,0:T(8,128)(2,1)}, bf16[80,1024]{1,0:T(8,128)(2,1)}, u32[]{:S(2)}, u32[]{:S(2)}) collective-permute-start(bf16[80,1024]{1,0:T(8,128)(2,1)} %get-tuple-element.60), channel_id=1, source_target_pairs={{0,15},{1,0},{2,1},{3,2},{4,3},{5,4},{6,5},{7,6},{8,7},{9,8},{10,9... | collective-permute-start | bytes 491528 | tf_op jit(solution)/shard_map/ppermute | solution.py:572
  22.6 12.6 %all-to-all-start = ((f32[256,4,128]{2,1,0:T(4,128)}), f32[256,4,128]{2,1,0:T(4,128)S(1)}, u32[]{:S(2)}, u32[]{:S(2)}) async-start(f32[256,4,128]{2,1,0:T(4,128)} %get-tuple-element.58), calls=%async_computation | async-start | bytes 1048576 | tf_op jit(solution)/shard_map/all_to_all | solution.py:544
  35.3 8.8 %shard_map.89 = (f32[384,768]{1,0:T(8,128)S(1)}, f32[192,256]{1,0:T(8,128)S(1)}, f32[96,256]{1,0:T(8,128)S(1)}, f32[48,256]{1,0:T(8,128)S(1)}) custom-call(s32[2]{0:T(128)S(1)} %pad_add_fusion.pos_ref, f32[6,384,128]{2,1,0:T(8,128)S(1)} %get-tuple-element.50.src_ref, f32[2,288,128]{2,1,0:T(8,128)S(1)} %get-tuple-element.51.a0, ...), custom_call_target="tpu_custom_call" | custom-call | flops 10000000000 | bytes 9912328 | tf_op jit(solution)/shard_map/pallas_call | solution.py:45
  46.4 9.5 %all-to-all-done = f32[256,4,128]{2,1,0:T(4,128)S(1)} async-done(((f32[256,4,128]{2,1,0:T(4,128)}), f32[256,4,128]{2,1,0:T(4,128)S(1)}, u32[]{:S(2)}, u32[]{:S(2)}) %all-to-all-start) | async-done | bytes 524320 | tf_op jit(solution)/shard_map/all_to_all | solution.py:544
  57.7 11.2 %shard_map.90 = (f32[384,768]{1,0:T(8,128)}, f32[6,384,128]{2,1,0:T(8,128)}, bf16[48,1536]{1,0:T(8,128)(2,1)S(1)}, bf16[48,1536]{1,0:T(8,128)(2,1)S(1)}, f32[256...) custom-call(s32[2]{0:T(128)S(1)} %pad_add_fusion.pos_ref, ...), custom_call_target="tpu_custom_call" | custom-call | flops 100000000 | bytes 7192840 | tf_op jit(solution)/shard_map/pallas_call | solution.py:45
  68.9 1.5 %collective-permute-start.4 = (bf16[48,1536]{1,0:T(8,128)(2,1)S(1)}, bf16[48,1536]{1,0:T(8,128)(2,1)S(1)}, u32[]{:S(2)}, u32[]{:S(2)}) collective-permute-start(bf16[48,1536]{1,0:T(8,128)(2,1)S(1)} %get-tuple-element.74), channel_id=1, source_target_pairs={{0,16},{16,32},{32,48},{48,64},{64,80},{80,96},{96,112},{112,128},... | collective-permute-start | bytes 442376 | tf_op jit(solution)/shard_map/ppermute | solution.py:564
  70.4 2.1 %collective-permute-done.4.above_ref = bf16[48,1536]{1,0:T(8,128)(2,1)S(1)} collective-permute-done((bf16[48,1536]{1,0:T(8,128)(2,1)S(1)}, bf16[48,1536]{1,0:T(8,128)(2,1)S(1)}, u32[]{:S(2)}, u32[]{:S(2)}) %collective-permute-start.4) | collective-permute-done | bytes 147488 | tf_op jit(solution)/shard_map/ppermute | solution.py:564
  72.5 2.7 %collective-permute-done.5.below_ref = bf16[48,1536]{1,0:T(8,128)(2,1)S(1)} collective-permute-done((bf16[48,1536]{1,0:T(8,128)(2,1)S(1)}, bf16[48,1536]{1,0:T(8,128)(2,1)S(1)}, u32[]{:S(2)}, u32[]{:S(2)}) %collective-permute-start.5) | collective-permute-done | bytes 147488 | tf_op jit(solution)/shard_map/ppermute | solution.py:565
  75.2 1.3 copy-done.5
  76.5 1.4 shard_map.91
  78.3 4.5 %collective-permute-start.7 = (bf16[80,1024]{1,0:T(8,128)(2,1)}, bf16[80,1024]{1,0:T(8,128)(2,1)}, u32[]{:S(2)}, u32[]{:S(2)}) collective-permute-start(bf16[80,1024]{1,0:T(8,128)(2,1)} %get-tuple-element.81), channel_id=1, source_target_pairs={{0,15},{1,0},{2,1},{3,2},{4,3},{5,4},{6,5},{7,6},{8,7},{9,8},{10,9... | collective-permute-start | bytes 491528 | tf_op jit(solution)/shard_map/ppermute | solution.py:572
  82.8 6.0 %all-to-all-start.1 = ((f32[256,4,128]{2,1,0:T(4,128)}), f32[256,4,128]{2,1,0:T(4,128)S(1)}, u32[]{:S(2)}, u32[]{:S(2)}) async-start(f32[256,4,128]{2,1,0:T(4,128)} %get-tuple-element.78), calls=%async_computation.1 | async-start | bytes 1048576 | tf_op jit(solution)/shard_map/all_to_all | solution.py:544
  91.6 8.8 %shard_map.92 = (f32[384,768]{1,0:T(8,128)S(1)}, f32[192,256]{1,0:T(8,128)S(1)}, f32[96,256]{1,0:T(8,128)S(1)}, f32[48,256]{1,0:T(8,128)S(1)}) custom-call(s32[2]{0:T(128)S(1)} %pad_add_fusion.pos_ref, f32[6,384,128]{2,1,0:T(8,128)S(1)} %copy-done.6, f32[2,288,128]{2,1,0:T(8,128)S(1)} %get-tuple-element.71.a0, f32[2,192,128]{2,1,0:T(8,128)S(1)} %get-tuple-element.72.a1, ...), custom_call_target="tpu_custom_call" | custom-call | flops 10000000000 | bytes 9912328 | tf_op jit(solution)/shard_map/pallas_call | solution.py:45
  102.7 6.9 %all-to-all-done.1 = f32[256,4,128]{2,1,0:T(4,128)S(1)} async-done(((f32[256,4,128]{2,1,0:T(4,128)}), f32[256,4,128]{2,1,0:T(4,128)S(1)}, u32[]{:S(2)}, u32[]{:S(2)}) %all-to-all-start.1) | async-done | bytes 524320 | tf_op jit(solution)/shard_map/all_to_all | solution.py:544
  111.5 9.6 %shard_map.93 = (f32[384,768]{1,0:T(8,128)S(1)}, f32[256,1,128]{2,1,0:T(1,128)S(1)}, f32[8,128]{1,0:T(8,128)S(1)}) custom-call(s32[2]{0:T(128)S(1)} %pad_add_fusion.pos_ref, f32[1024,128]{1,0:T(8,128)S(1)} %bitcast.20, f32[1024,128]{1,0:T(8,128)S(1)} %bitcast.19, f32[384,768]{1,0:T(8,128)} %bitcast.16, f32[384,768]{1,0:T(8,128)} %get-tuple-element.79.u_ref, ...), custom_call_target="tpu_custom_call" | custom-call | flops 100000000 | bytes 8830984 | tf_op jit(solution)/shard_map/pallas_call | solution.py:45
  121.1 19.8 %all_to_all.15 = f32[256,1,128]{2,1,0:T(1,128)S(1)} all-to-all(f32[256,1,128]{2,1,0:T(1,128)S(1)} %get-tuple-element.87), channel_id=1, replica_groups=mesh['z'=8,'c'=2,'y'=4,'x1'=2,'x0'=2] {'c','x0','z','y','x1'}, dimensions={0} | all-to-all | bytes 262144 | tf_op jit(solution)/shard_map/all_to_all | solution.py:544
  140.9 1.8 %shard_map.94 = (f32[384,768]{1,0:T(8,128)}, f32[6,6]{1,0:T(8,128)}) custom-call(f32[256,128]{1,0:T(8,128)S(1)} %bitcast.24, f32[8,128]{1,0:T(8,128)S(1)} %get-tuple-element.88.totals_ref, f32[384,768]{1,0:T(8,128)S(1)} %bitcast.17, f32[384,768]{1,0:T(8,128)S(1)} %copy-done.2, f32[384,768]{1,0:T(8,128)S(1)} %get-tuple-element.89.v_ref), custom_call_target="tpu_custom_call" | custom-call | flops 1000000 | bytes 3674112 | tf_op jit(solution)/shard_map/pallas_call | solution.py:45
  (58 shorter events, 12.7 us)
Async XLA Ops:
  0.6 1.7 %copy-start.23 = (s32[8,8]{1,0:T(8,128)S(1)}, s32[8,8]{1,0:T(8,128)}, u32[]{:S(2)}) copy-start(s32[8,8]{1,0:T(8,128)} %occupied_ref.3) | copy-start | bytes 772
  0.6 1.7 %copy-start.7 = (bf16[768,64]{0,1:T(8,128)(2,1)S(1)}, bf16[768,64]{0,1:T(8,128)(2,1)}, u32[]{:S(2)}) copy-start(bf16[768,64]{0,1:T(8,128)(2,1)} %param.11) | copy-start | bytes 294916
  0.7 1.7 %copy-start.8 = (f32[8,8,256]{2,1,0:T(8,128)S(1)}, f32[8,8,256]{2,1,0:T(8,128)}, u32[]{:S(2)}) copy-start(f32[8,8,256]{2,1,0:T(8,128)} %param.8) | copy-start | bytes 196612
  6.3 10.1 %collective-permute-start = (bf16[48,1536]{1,0:T(8,128)(2,1)S(1)}, bf16[48,1536]{1,0:T(8,128)(2,1)S(1)}, u32[]{:S(2)}, u32[]{:S(2)}) collective-permute-start(bf16[48,1536]{1,0:T(8,128)(2,1)S(1)} %get-tuple-element.54), channel_id=1, source_target_pairs={{0,16},{16,32},{32,48},{48,64},{64,80},{80,96},{96,112},{112,128},... | collective-permute-start | bytes 442376 | tf_op jit(solution)/shard_map/ppermute | solution.py:564
  9.3 7.1 %collective-permute-start.1 = (bf16[48,1536]{1,0:T(8,128)(2,1)S(1)}, bf16[48,1536]{1,0:T(8,128)(2,1)S(1)}, u32[]{:S(2)}, u32[]{:S(2)}) collective-permute-start(bf16[48,1536]{1,0:T(8,128)(2,1)S(1)} %get-tuple-element.55), channel_id=1, source_target_pairs={{0,240},{16,0},{32,16},{48,32},{64,48},{80,64},{96,80},{112,96},{1... | collective-permute-start | bytes 442376 | tf_op jit(solution)/shard_map/ppermute | solution.py:565
  14.0 1.2 copy-start.1
  15.2 1.2 copy-start.24
  17.8 17.4 %collective-permute-start.2 = (bf16[80,1024]{1,0:T(8,128)(2,1)}, bf16[80,1024]{1,0:T(8,128)(2,1)}, u32[]{:S(2)}, u32[]{:S(2)}) collective-permute-start(bf16[80,1024]{1,0:T(8,128)(2,1)} %get-tuple-element.59), channel_id=1, source_target_pairs={{0,1},{1,2},{2,3},{3,4},{4,5},{5,6},{6,7},{7,8},{8,9},{9,10},{10,1... | collective-permute-start | bytes 491528 | tf_op jit(solution)/shard_map/ppermute | solution.py:573
  18.8 16.4 %collective-permute-start.3 = (bf16[80,1024]{1,0:T(8,128)(2,1)}, bf16[80,1024]{1,0:T(8,128)(2,1)}, u32[]{:S(2)}, u32[]{:S(2)}) collective-permute-start(bf16[80,1024]{1,0:T(8,128)(2,1)} %get-tuple-element.60), channel_id=1, source_target_pairs={{0,15},{1,0},{2,1},{3,2},{4,3},{5,4},{6,5},{7,6},{8,7},{9,8},{10,9... | collective-permute-start | bytes 491528 | tf_op jit(solution)/shard_map/ppermute | solution.py:572
  22.6 33.3 %all-to-all-start = ((f32[256,4,128]{2,1,0:T(4,128)}), f32[256,4,128]{2,1,0:T(4,128)S(1)}, u32[]{:S(2)}, u32[]{:S(2)}) async-start(f32[256,4,128]{2,1,0:T(4,128)} %get-tuple-element.58), calls=%async_computation | async-start | bytes 1048576 | tf_op jit(solution)/shard_map/all_to_all | solution.py:544
  44.1 1.0 copy-start.4
  68.9 9.0 %copy-start.13 = (f32[2,144,128]{2,1,0:T(8,128)}, f32[2,144,128]{2,1,0:T(8,128)S(1)}, u32[]{:S(2)}) copy-start(f32[2,144,128]{2,1,0:T(8,128)S(1)} %get-tuple-element.73.a2) | copy-start | bytes 442372
  68.9 3.6 %collective-permute-start.4 = (bf16[48,1536]{1,0:T(8,128)(2,1)S(1)}, bf16[48,1536]{1,0:T(8,128)(2,1)S(1)}, u32[]{:S(2)}, u32[]{:S(2)}) collective-permute-start(bf16[48,1536]{1,0:T(8,128)(2,1)S(1)} %get-tuple-element.74), channel_id=1, source_target_pairs={{0,16},{16,32},{32,48},{48,64},{64,80},{80,96},{96,112},{112,128},... | collective-permute-start | bytes 442376 | tf_op jit(solution)/shard_map/ppermute | solution.py:564
  70.4 4.8 %collective-permute-start.5 = (bf16[48,1536]{1,0:T(8,128)(2,1)S(1)}, bf16[48,1536]{1,0:T(8,128)(2,1)S(1)}, u32[]{:S(2)}, u32[]{:S(2)}) collective-permute-start(bf16[48,1536]{1,0:T(8,128)(2,1)S(1)} %get-tuple-element.75), channel_id=1, source_target_pairs={{0,240},{16,0},{32,16},{48,32},{64,48},{80,64},{96,80},{112,96},{1... | collective-permute-start | bytes 442376 | tf_op jit(solution)/shard_map/ppermute | solution.py:565
  72.5 5.4 %copy-start.15 = (bf16[48,1536]{1,0:T(8,128)(2,1)}, bf16[48,1536]{1,0:T(8,128)(2,1)S(1)}, u32[]{:S(2)}) copy-start(bf16[48,1536]{1,0:T(8,128)(2,1)S(1)} %collective-permute-done.4.above_ref) | copy-start | bytes 442372
  75.2 2.7 %copy-start.17 = (bf16[48,1536]{1,0:T(8,128)(2,1)}, bf16[48,1536]{1,0:T(8,128)(2,1)S(1)}, u32[]{:S(2)}) copy-start(bf16[48,1536]{1,0:T(8,128)(2,1)S(1)} %collective-permute-done.5.below_ref) | copy-start | bytes 442372
  75.2 1.3 copy-start.5
  76.5 12.3 %copy-start.6 = (f32[6,384,128]{2,1,0:T(8,128)S(1)}, f32[6,384,128]{2,1,0:T(8,128)}, u32[]{:S(2)}) copy-start(f32[6,384,128]{2,1,0:T(8,128)} %get-tuple-element.70.src_ref) | copy-start | bytes 3538948
  77.9 10.9 %collective-permute-start.6 = (bf16[80,1024]{1,0:T(8,128)(2,1)}, bf16[80,1024]{1,0:T(8,128)(2,1)}, u32[]{:S(2)}, u32[]{:S(2)}) collective-permute-start(bf16[80,1024]{1,0:T(8,128)(2,1)} %get-tuple-element.80), channel_id=1, source_target_pairs={{0,1},{1,2},{2,3},{3,4},{4,5},{5,6},{6,7},{7,8},{8,9},{9,10},{10,1... | collective-permute-start | bytes 491528 | tf_op jit(solution)/shard_map/ppermute | solution.py:573
  78.3 10.5 %collective-permute-start.7 = (bf16[80,1024]{1,0:T(8,128)(2,1)}, bf16[80,1024]{1,0:T(8,128)(2,1)}, u32[]{:S(2)}, u32[]{:S(2)}) collective-permute-start(bf16[80,1024]{1,0:T(8,128)(2,1)} %get-tuple-element.81), channel_id=1, source_target_pairs={{0,15},{1,0},{2,1},{3,2},{4,3},{5,4},{6,5},{7,6},{8,7},{9,8},{10,9... | collective-permute-start | bytes 491528 | tf_op jit(solution)/shard_map/ppermute | solution.py:572
  82.8 26.8 %all-to-all-start.1 = ((f32[256,4,128]{2,1,0:T(4,128)}), f32[256,4,128]{2,1,0:T(4,128)S(1)}, u32[]{:S(2)}, u32[]{:S(2)}) async-start(f32[256,4,128]{2,1,0:T(4,128)} %get-tuple-element.78), calls=%async_computation.1 | async-start | bytes 1048576 | tf_op jit(solution)/shard_map/all_to_all | solution.py:544
  100.4 1.0 copy-start.3
  111.5 29.5 %copy-start = (f32[8,8,6,3,256]{4,1,3,2,0:T(8,128)S(1)}, f32[8,8,6,3,256]{4,1,3,2,0:T(8,128)}, u32[]{:S(2)}) copy-start(f32[8,8,6,3,256]{4,1,3,2,0:T(8,128)} %param.7) | copy-start | bytes 3538948
  111.5 29.5 %copy-start.2 = (f32[384,768]{1,0:T(8,128)S(1)}, f32[384,768]{1,0:T(8,128)}, u32[]{:S(2)}) copy-start(f32[384,768]{1,0:T(8,128)} %get-tuple-element.79.u_ref) | copy-start | bytes 3538948
  (11 other events, 9.0 us)
where the time goes:
time: 143 us
  Pallas kernels  51.3 us (36%)
  starting transfers between devices  33.1 us (23%)
  waiting for transfers between devices  21.2 us (15%)
  blocking collectives  19.8 us (14%)
  local copies, waits for them, and re-layouts  14.7 us (10%)
  other arithmetic  1.78 us (1%)
    pallas_call x9, Pallas kernels, call(): pl.pallas_call(kernel, out_shape=outs, in_specs=specs, out_specs=jax.tree...  51.3 us
    all_to_all x1, blocking collectives, to_everyone(): return lax.all_to_all(blocks, CLASS_ORDER, 0, 0, tiled=True)  19.8 us
    all_to_all x2, starting transfers between devices, to_everyone(): return lax.all_to_all(blocks, CLASS_ORDER, 0, 0, tiled=True)  18.6 us
    all_to_all x2, waiting for transfers between devices, to_everyone(): return lax.all_to_all(blocks, CLASS_ORDER, 0, 0, tiled=True)  16.4 us
    unnamed x50, local copies, waits for them, and re-layouts  14.7 us
    ppermute x2, starting transfers between devices, exchange(): right = lax.ppermute(to_left, GY, turn(16, -1))  8.27 us
    ppermute x2, starting transfers between devices, exchange(): above = lax.ppermute(up, GX, turn(16, 1))  4.54 us
  transfers between devices with their start and end apart: 10, of which 4 were waited for; matrix products, arithmetic and copies ran while one was open for 0% of the time, Pallas kernels for 16%

commit v1 on v0

--- a/solution.py
+++ b/solution.py
@@ -53,9 +53,9 @@
     )(*args)
 
 
-def pair_blocks(coupling_ref, inner_ref, high_ref, low_ref):
+def pair_blocks(first, coupling_ref, *out_refs):
     zero = jnp.zeros((64, 64), F32)
-    for level in range(6):
+    for level in range(3):
         flipped = {}
         for n, (dp, dq) in enumerate(HALF):
             for c_in, e_in in CHILDREN:
@@ -66,21 +66,19 @@
                         if max(abs(d[0]), abs(d[1])) < 2:
                             row.append(zero)
                         elif d in FAR:
-                            row.append(coupling_ref[level, FAR.index(d)])
+                            row.append(coupling_ref[first + level, FAR.index(d)])
                         else:
                             k = FAR.index((-d[0], -d[1]))
                             if k not in flipped:
-                                flipped[k] = coupling_ref[level, k].T
+                                flipped[k] = coupling_ref[first + level, k].T
                             row.append(flipped[k])
                     r0 = (2 * c_in + e_in) * 64
                     rows, lanes = slice(r0, r0 + 64), slice(c * 128, c * 128 + 128)
                     block = jnp.concatenate(row, axis=1)
                     high = block.astype(BF16)
-                    if level < 3:
-                        inner_ref[level, n, rows, lanes] = high
-                    else:
-                        high_ref[level - 3, n, rows, lanes] = high
-                        low_ref[level - 3, n, rows, lanes] = (block - high.astype(F32)).astype(BF16)
+                    out_refs[0][level, n, rows, lanes] = high
+                    if len(out_refs) > 1:
+                        out_refs[1][level, n, rows, lanes] = (block - high.astype(F32)).astype(BF16)
 
 
 def in_two(x):
@@ -131,9 +129,22 @@
     return jnp.concatenate([ref[t, rows, :] for t in range(ref.shape[0])], axis=1)
 
 
+def doubled(x):
+    return jnp.concatenate([x, x], axis=1)
+
+
+def levels_of(ref):
+    return [ref.at[:, 0:288, :], ref.at[:, 288:480, :], ref.at[:, 480:624, :]]
+
+
+def inner_parts(ref):
+    return [ref.at[0:192, :], ref.at[192:288, :], ref.at[288:336, :]]
+
+
 def spread_skeleton(field_at, sums_row, refs, skel):
     contrast_ref, occupied_ref, basis_ref, transfer_ref = refs[0]
-    src_ref, up_ref, down_ref, pay_ref, *tree = refs[1]
+    src_ref, up_ref, down_ref, pay_ref, tree_ref = refs[1]
+    tree = levels_of(tree_ref)
     twice = jnp.concatenate([basis_ref[...]] * 2, axis=0)
     for i in range(8):
         rows = slice(48 * i, 48 * i + 48)
@@ -161,7 +172,7 @@
         down_ref[:, lanes] = tiles(node, slice(48, 96)).astype(BF16)
         skel[0 : 48 * n, :] = jnp.dot(
             tiles(node, slice(48, 48 * n + 48)),
-            transfer_ref[level],
+            doubled(transfer_ref[level]),
             precision=EXACT,
             preferred_element_type=F32,
         )
@@ -175,15 +186,13 @@
     jax.ShapeDtypeStruct((48, 1536), BF16),
     jax.ShapeDtypeStruct((48, 1536), BF16),
     jax.ShapeDtypeStruct((256, 4, 128), F32),
-    jax.ShapeDtypeStruct((2, 288, 128), F32),
-    jax.ShapeDtypeStruct((2, 192, 128), F32),
-    jax.ShapeDtypeStruct((2, 144, 128), F32),
+    jax.ShapeDtypeStruct((2, 624, 128), F32),
 ]
 SOURCE_SCRATCH = [pltpu.VMEM((384, 128), F32)]
 
 
 def first_source(x_ref, contrast_ref, occupied_ref, basis_ref, transfer_ref, *rest):
-    outs, skel = rest[:7], rest[7]
+    outs, skel = rest[:5], rest[5]
     acc = jnp.zeros((48, 128), F32)
     for i in range(8):
         x = x_ref[48 * i : 48 * i + 48, :]
@@ -196,7 +205,7 @@
     )
 
 
-def columns(pos_ref, src_ref, a0, a1, a2, above_ref, below_ref, left_ref, right_ref, above, below):
+def columns(pos_ref, src_ref, tree_ref, above_ref, below_ref, left_ref, right_ref, above, below):
     gx = pos_ref[0]
     for t in range(12):
         lanes = slice(128 * t, 128 * t + 128)
@@ -216,7 +225,7 @@
             out[60:80, 128 * t : 128 * t + 128] = jnp.zeros((20, 128), BF16)
         for t in range(2):
             parts = []
-            for level, (node, n) in enumerate(zip((a0, a1, a2), PARENTS)):
+            for level, (node, n) in enumerate(zip(levels_of(tree_ref), PARENTS)):
                 q = n if side else 1
                 parts += [
                     above[6 + 2 * level + t, pl.ds(q, 6, stride=8), :],
@@ -228,8 +237,8 @@
 
 
 def near_and_low(
-    pos_ref, src_ref, a0, a1, a2, above_ref, below_ref, left_ref, right_ref, near_ref, inner_ref,
-    near_out, o0, o1, o2, wide, moved, edge, placed, n0, n1, n2, turned,
+    pos_ref, src_ref, tree_ref, above_ref, below_ref, left_ref, right_ref, near_ref, inner_ref,
+    near_out, inner_out, wide, moved, edge, placed, n0, n1, n2, turned,
 ):
     gx, gy = pos_ref[0], pos_ref[1]
     up = (gx > 0).astype(F32)
@@ -270,7 +279,7 @@
                 near_out[...] += part
     start = 0
     for level, (node, full, out, n) in enumerate(
-        zip((a0, a1, a2), (n0, n1, n2), (o0, o1, o2), PARENTS)
+        zip(levels_of(tree_ref), (n0, n1, n2), inner_parts(inner_out), PARENTS)
     ):
         size, lanes = 48 * (n + 2), slice(768 + 256 * level, 1024 + 256 * level)
         for t in range(2):
@@ -360,7 +369,7 @@
                 ]
         lifted = jnp.dot(
             side_by[0 : 6 * m, :],
-            transfer_ref[3 + step, :, 0:64],
+            transfer_ref[3 + step],
             precision=EXACT,
             preferred_element_type=F32,
         )
@@ -377,17 +386,18 @@
 
     reached = own_child(outs[2], 2)
     for step in (1, 0):
-        reached = own_child(outs[step] + dot_t(reached, transfer_ref[3 + step, :, 0:64], EXACT), step)
+        reached = own_child(outs[step] + dot_t(reached, transfer_ref[3 + step], EXACT), step)
     return jnp.concatenate([reached, jnp.zeros((8, 64), F32)], axis=1)
 
 
-def far_down(reached, o0, o1, o2, transfer_ref, flat, held):
+def far_down(reached, inner_ref, transfer_ref, flat, held):
+    o0, o1, o2 = inner_parts(inner_ref)
     half = left_half((6, 128))
     flat[...] = jnp.zeros(flat.shape, F32)
     flat[pl.ds(1, 8, stride=8), :] = reached
     for level, out in ((2, o2), (1, o1), (0, o0)):
         n = PARENTS[level]
-        value = out[...] + dot_t(flat[0 : 48 * n, :], transfer_ref[level], EXACT)
+        value = out[...] + dot_t(flat[0 : 48 * n, :], doubled(transfer_ref[level]), EXACT)
         for t in range(2):
             held[t, 0 : 48 * n, :] = value[:, 128 * t : 128 * t + 128]
         offset = min(level, 1)
@@ -429,12 +439,12 @@
 
 
 def second_source(
-    pos_ref, all_ref, x_ref, near_ref, o0, o1, o2, high_ref, low_ref, contrast_ref, occupied_ref, basis_ref,
+    pos_ref, all_ref, x_ref, near_ref, inner_ref, high_ref, low_ref, contrast_ref, occupied_ref, basis_ref,
     transfer_ref, u_ref, *rest,
 ):
-    outs, (by_child, grown, side_by, flat, held, skel) = rest[:7], rest[7:]
+    outs, (by_child, grown, side_by, flat, held, skel) = rest[:5], rest[5:]
     reached = far_above(pos_ref, all_ref, (high_ref, low_ref), transfer_ref, by_child, grown, side_by)
-    far_down(reached, o0, o1, o2, transfer_ref, flat, held)
+    far_down(reached, inner_ref, transfer_ref, flat, held)
     cross = jnp.zeros((48, 128), F32)
     square = jnp.zeros((48, 128), F32)
     for i in range(8):
@@ -471,7 +481,7 @@
 
 
 def last_sums(
-    count, pos_ref, all_ref, before_ref, x_ref, u_ref, near_ref, o0, o1, o2, high_ref, low_ref, basis_ref,
+    count, pos_ref, all_ref, before_ref, x_ref, u_ref, near_ref, inner_ref, high_ref, low_ref, basis_ref,
     transfer_ref, v_ref, sums_ref, totals_ref, by_child, grown, side_by, flat, held,
 ):
     first_totals, second_totals = totals_of(before_ref), totals_of(all_ref)
@@ -480,7 +490,7 @@
     k = scales(first_totals, second_totals, count)
     over, over_two = 1.0 / k["beta"], 1.0 / k["h21"]
     reached = far_above(pos_ref, all_ref, (high_ref, low_ref), transfer_ref, by_child, grown, side_by)
-    far_down(reached, o0, o1, o2, transfer_ref, flat, held)
+    far_down(reached, inner_ref, transfer_ref, flat, held)
     sums = [jnp.zeros((48, 128), F32)] * 3
     for i in range(8):
         rows = slice(48 * i, 48 * i + 48)
@@ -550,23 +560,26 @@
     x = rhs.transpose(0, 2, 1, 3, 4).reshape(384, 768)
     contrast = contrast.reshape(64, voxels)
     stacked = transfer.reshape(5, 256, 64)
-    stacked = jnp.concatenate([stacked] * 2, axis=2)
     basis = basis.T
     pos = jnp.stack([lax.axis_index(GX), lax.axis_index(GY)]).astype(jnp.int32)
     shape = jax.ShapeDtypeStruct
-    inner, *outer = call(
-        pair_blocks, [shape((3, 4, 256, 256), BF16)] * 3, [VMEM], [], 10**8, coupling
+    blocks = shape((3, 4, 256, 256), BF16)
+    (inner,) = call(
+        functools.partial(pair_blocks, 0), [blocks], [VMEM], [], 10**8, coupling
+    )
+    outer = call(
+        functools.partial(pair_blocks, 3), [blocks] * 2, [VMEM], [], 10**8, coupling
     )
 
     def exchange(outs, inner):
-        src, up, down, pay, a0, a1, a2 = outs
+        src, up, down, pay, tree = outs
         src, inner = lax.optimization_barrier((src, inner))
         above = lax.ppermute(up, GX, turn(16, 1))
         below = lax.ppermute(down, GX, turn(16, -1))
         to_left, to_right = call(
-            columns, [shape((80, 1024), BF16)] * 2, [SMEM] + [VMEM] * 6,
+            columns, [shape((80, 1024), BF16)] * 2, [SMEM] + [VMEM] * 4,
             [pltpu.VMEM((12, 48, 128), F32)] * 2, 10**6,
-            pos, src, a0, a1, a2, above, below,
+            pos, src, tree, above, below,
         )
         pay, to_left, to_right = lax.optimization_barrier((pay, to_left, to_right))
         right = lax.ppermute(to_left, GY, turn(16, -1))
@@ -574,15 +587,15 @@
         everyone = to_everyone(pay).reshape(1024, 128)
         parts = call(
             near_and_low,
-            [shape((384, 768), F32), shape((192, 256), F32), shape((96, 256), F32), shape((48, 256), F32)],
-            [SMEM] + [VMEM] * 10,
+            [shape((384, 768), F32), shape((336, 256), F32)],
+            [SMEM] + [VMEM] * 8,
             [
                 pltpu.VMEM((6, 480, 128), F32), pltpu.VMEM((6, 480, 128), F32), pltpu.VMEM((80, 768), F32),
                 pltpu.VMEM((480, 768), BF16), pltpu.VMEM((2, 288, 128), F32), pltpu.VMEM((2, 192, 128), F32),
                 pltpu.VMEM((2, 144, 128), F32), pltpu.VMEM((288, 256), F32),
             ],
             10**10,
-            pos, src, a0, a1, a2, above, below, left, right, near, inner,
+            pos, src, tree, above, below, left, right, near, inner,
         )
         return everyone, parts
 
@@ -592,7 +605,7 @@
     )
     all_one, parts = exchange(outs, inner)
     u, *outs = call(
-        second_source, [shape((384, 768), F32)] + SOURCE_OUTS, [SMEM] + [VMEM] * 12,
+        second_source, [shape((384, 768), F32)] + SOURCE_OUTS, [SMEM] + [VMEM] * 10,
         FAR_SCRATCH + SOURCE_SCRATCH, 10**8,
         pos, all_one, x, *parts, *outer, contrast, occupied, basis, stacked,
     )
@@ -600,7 +613,7 @@
     v, sums, totals = call(
         functools.partial(last_sums, count),
         [shape((384, 768), F32), shape((256, 1, 128), F32), shape((8, 128), F32)],
-        [SMEM] + [VMEM] * 12, FAR_SCRATCH, 10**8,
+        [SMEM] + [VMEM] * 10, FAR_SCRATCH, 10**8,
         pos, all_two, all_one, x, u, *parts, *outer, basis, stacked,
     )
     third, hess = call(

time: 143 us -> 138 us (0.965)
  waiting for transfers between devices: 21.2 us -> 17 us
  other arithmetic: 1.78 us -> 0.07 us
    all_to_all x2, waiting for transfers between devices: 16.4 us -> 11.4 us  [to_everyone(): return lax.all_to_all(blocks, CLASS_ORDER, 0, 0, tiled=True)]
    concatenate x1 -> x0, other arithmetic: 1.7 us -> none  [body(): stacked = jnp.concatenate([stacked] * 2, axis=2)]
    pallas_call x9 -> x10, Pallas kernels: 51.3 us -> 52.1 us  [call(): pl.pallas_call(kernel, out_shape=outs, in_specs=specs, out_specs=jax.tree...]
    unnamed x50 -> x54, local copies, waits for them, and re-layouts: 14.7 us -> 15.5 us
  transfers between devices with their start and end apart: 10 -> 10, of which waited for: 4 -> 5; matrix products, arithmetic and copies ran while one was open for 0% -> 0% of each run, Pallas kernels for 16% -> 17%
where the time goes in v1:
time: 138 us; the launch traced here: 137 us
  Pallas kernels  52.1 us (38%)
  starting transfers between devices  32.5 us (24%)
  blocking collectives  19.2 us (14%)
  waiting for transfers between devices  17 us (12%)
  local copies, waits for them, and re-layouts  15.5 us (11%)
    pallas_call x10, Pallas kernels, call(): pl.pallas_call(kernel, out_shape=outs, in_specs=specs, out_specs=jax.tree...  52.1 us
    all_to_all x1, blocking collectives, to_everyone(): return lax.all_to_all(blocks, CLASS_ORDER, 0, 0, tiled=True)  19.2 us
    all_to_all x2, starting transfers between devices, to_everyone(): return lax.all_to_all(blocks, CLASS_ORDER, 0, 0, tiled=True)  18.1 us
    unnamed x54, local copies, waits for them, and re-layouts  15.5 us
    all_to_all x2, waiting for transfers between devices, to_everyone(): return lax.all_to_all(blocks, CLASS_ORDER, 0, 0, tiled=True)  11.4 us
    ppermute x2, starting transfers between devices, exchange(): right = lax.ppermute(to_left, GY, turn(16, -1))  8.21 us
    ppermute x2, starting transfers between devices, exchange(): above = lax.ppermute(up, GX, turn(16, 1))  4.55 us
    ppermute x2, waiting for transfers between devices, exchange(): below = lax.ppermute(down, GX, turn(16, -1))  3.49 us
  transfers between devices with their start and end apart: 10, of which 5 were waited for; matrix products, arithmetic and copies ran while one was open for 0% of the time, Pallas kernels for 17%

profile of v1, /device:TPU:1, one launch (start us, length us, event | category | flops | bytes accessed | tf_op | source)
XLA Modules:
  0.0 137.3 jit_solution(17351707105536271276)
XLA Ops:
  4.1 3.9 %shard_map.86 = (f32[6,384,128]{2,1,0:T(8,128)S(1)}, bf16[48,1536]{1,0:T(8,128)(2,1)S(1)}, bf16[48,1536]{1,0:T(8,128)(2,1)S(1)}, f32[256,4,128]{2,1,0:T(4,128)}, f32[2,624,128]{2,1,0:T(8,128)S(1)}) custom-call(f32[384,768]{1,0:T(8,128)} %bitcast.14, f32[64,256]{1,0:T(8,128)S(1)} %bitcast.28, s32[8,8]{1,0:T(8,128)S(1)} %copy-done.21, ...), custom_call_target="tpu_custom_call" | custom-call | flops 100000000 | bytes 1671424 | tf_op jit(solution)/shard_map/pallas_call | solution.py:45
  8.0 3.0 %collective-permute-start = (bf16[48,1536]{1,0:T(8,128)(2,1)S(1)}, bf16[48,1536]{1,0:T(8,128)(2,1)S(1)}, u32[]{:S(2)}, u32[]{:S(2)}) collective-permute-start(bf16[48,1536]{1,0:T(8,128)(2,1)S(1)} %get-tuple-element.42), channel_id=1, source_target_pairs={{0,16},{16,32},{32,48},{48,64},{64,80},{80,96},{96,112},{112,128},... | collective-permute-start | bytes 442376 | tf_op jit(solution)/shard_map/ppermute | solution.py:577
  11.3 2.6 %shard_map.87.inner_ref = bf16[3,4,256,256]{3,2,1,0:T(8,128)(2,1)S(1)} custom-call(f32[6,20,64,64]{3,2,1,0:T(8,128)} %coupling_ref.3), custom_call_target="tpu_custom_call" | custom-call | flops 100000000 | bytes 1966080 | tf_op jit(solution)/shard_map/pallas_call | solution.py:45
  13.9 1.2 copy-done.6
  15.9 1.4 %shard_map.88 = (bf16[80,1024]{1,0:T(8,128)(2,1)S(1)}, bf16[80,1024]{1,0:T(8,128)(2,1)}) custom-call(s32[2]{0:T(128)S(1)} %pad_add_fusion.pos_ref, f32[6,384,128]{2,1,0:T(8,128)S(1)} %get-tuple-element.40.src_ref, f32[2,624,128]{2,1,0:T(8,128)S(1)} %get-tuple-element.41.tree_ref, bf16[48,1536]{1,0:T(8,128)(2,1)S(1)} %collective-permute-done.above_ref, ...), custom_call_target="tpu_custom_call" | custom-call | flops 1000000 | bytes 2113544 | tf_op jit(solution)/shard_map/pallas_call | solution.py:45
  17.3 1.2 collective-permute-start.2
  18.5 3.7 %collective-permute-start.3 = (bf16[80,1024]{1,0:T(8,128)(2,1)S(1)}, bf16[80,1024]{1,0:T(8,128)(2,1)S(1)}, u32[]{:S(2)}, u32[]{:S(2)}) collective-permute-start(bf16[80,1024]{1,0:T(8,128)(2,1)S(1)} %get-tuple-element.48), channel_id=1, source_target_pairs={{0,15},{1,0},{2,1},{3,2},{4,3},{5,4},{6,5},{7,6},{8,7},{9,8},{10,9... | collective-permute-start | bytes 491528 | tf_op jit(solution)/shard_map/ppermute | solution.py:585
  22.2 11.7 %all-to-all-start = ((f32[256,4,128]{2,1,0:T(4,128)}), f32[256,4,128]{2,1,0:T(4,128)S(1)}, u32[]{:S(2)}, u32[]{:S(2)}) async-start(f32[256,4,128]{2,1,0:T(4,128)} %get-tuple-element.46), calls=%async_computation | async-start | bytes 1048576 | tf_op jit(solution)/shard_map/all_to_all | solution.py:554
  33.9 3.0 %shard_map.90 = (bf16[3,4,256,256]{3,2,1,0:T(8,128)(2,1)S(1)}, bf16[3,4,256,256]{3,2,1,0:T(8,128)(2,1)S(1)}) custom-call(f32[6,20,64,64]{3,2,1,0:T(8,128)} %coupling_ref.3), custom_call_target="tpu_custom_call" | custom-call | flops 100000000 | bytes 1966080 | tf_op jit(solution)/shard_map/pallas_call | solution.py:45
  40.9 8.6 %shard_map.89 = (f32[384,768]{1,0:T(8,128)S(1)}, f32[336,256]{1,0:T(8,128)S(1)}) custom-call(s32[2]{0:T(128)S(1)} %pad_add_fusion.pos_ref, f32[6,384,128]{2,1,0:T(8,128)S(1)} %get-tuple-element.40.src_ref, f32[2,624,128]{2,1,0:T(8,128)S(1)} %copy-done.14, bf16[48,1536]{1,0:T(8,128)(2,1)S(1)} %collective-permute-done.above_ref, ...), custom_call_target="tpu_custom_call" | custom-call | flops 10000000000 | bytes 9912328 | tf_op jit(solution)/shard_map/pallas_call | solution.py:45
  50.5 4.0 %all-to-all-done = f32[256,4,128]{2,1,0:T(4,128)S(1)} async-done(((f32[256,4,128]{2,1,0:T(4,128)}), f32[256,4,128]{2,1,0:T(4,128)S(1)}, u32[]{:S(2)}, u32[]{:S(2)}) %all-to-all-start) | async-done | bytes 524320 | tf_op jit(solution)/shard_map/all_to_all | solution.py:554
  54.6 11.2 %shard_map.91 = (f32[384,768]{1,0:T(8,128)}, f32[6,384,128]{2,1,0:T(8,128)}, bf16[48,1536]{1,0:T(8,128)(2,1)S(1)}, bf16[48,1536]{1,0:T(8,128)(2,1)S(1)}, f32[256...) custom-call(s32[2]{0:T(128)S(1)} %pad_add_fusion.pos_ref, f32[1024,128]{1,0:T(8,128)S(1)} %bitcast.21, f32[384,768]{1,0:T(8,128)} %bitcast.15, ...), custom_call_target="tpu_custom_call" | custom-call | flops 100000000 | bytes 6865160 | tf_op jit(solution)/shard_map/pallas_call | solution.py:45
  65.8 1.5 %collective-permute-start.4 = (bf16[48,1536]{1,0:T(8,128)(2,1)S(1)}, bf16[48,1536]{1,0:T(8,128)(2,1)S(1)}, u32[]{:S(2)}, u32[]{:S(2)}) collective-permute-start(bf16[48,1536]{1,0:T(8,128)(2,1)S(1)} %get-tuple-element.58), channel_id=1, source_target_pairs={{0,16},{16,32},{32,48},{48,64},{64,80},{80,96},{96,112},{112,128},... | collective-permute-start | bytes 442376 | tf_op jit(solution)/shard_map/ppermute | solution.py:577
  67.3 2.1 %collective-permute-done.4.above_ref = bf16[48,1536]{1,0:T(8,128)(2,1)S(1)} collective-permute-done((bf16[48,1536]{1,0:T(8,128)(2,1)S(1)}, bf16[48,1536]{1,0:T(8,128)(2,1)S(1)}, u32[]{:S(2)}, u32[]{:S(2)}) %collective-permute-start.4) | collective-permute-done | bytes 147488 | tf_op jit(solution)/shard_map/ppermute | solution.py:577
  69.4 2.7 %collective-permute-done.5.below_ref = bf16[48,1536]{1,0:T(8,128)(2,1)S(1)} collective-permute-done((bf16[48,1536]{1,0:T(8,128)(2,1)S(1)}, bf16[48,1536]{1,0:T(8,128)(2,1)S(1)}, u32[]{:S(2)}, u32[]{:S(2)}) %collective-permute-start.5) | collective-permute-done | bytes 147488 | tf_op jit(solution)/shard_map/ppermute | solution.py:578
  72.1 1.3 copy-done.9
  73.4 1.4 %shard_map.92 = (bf16[80,1024]{1,0:T(8,128)(2,1)}, bf16[80,1024]{1,0:T(8,128)(2,1)}) custom-call(s32[2]{0:T(128)S(1)} %pad_add_fusion.pos_ref, f32[6,384,128]{2,1,0:T(8,128)S(1)} %copy-done.9, f32[2,624,128]{2,1,0:T(8,128)S(1)} %get-tuple-element.57.tree_ref, bf16[48,1536]{1,0:T(8,128)(2,1)S(1)} %collective-permute-done.4.above_ref, ...), custom_call_target="tpu_custom_call" | custom-call | flops 1000000 | bytes 2113544 | tf_op jit(solution)/shard_map/pallas_call | solution.py:45
  75.2 4.5 %collective-permute-start.7 = (bf16[80,1024]{1,0:T(8,128)(2,1)}, bf16[80,1024]{1,0:T(8,128)(2,1)}, u32[]{:S(2)}, u32[]{:S(2)}) collective-permute-start(bf16[80,1024]{1,0:T(8,128)(2,1)} %get-tuple-element.65), channel_id=1, source_target_pairs={{0,15},{1,0},{2,1},{3,2},{4,3},{5,4},{6,5},{7,6},{8,7},{9,8},{10,9... | collective-permute-start | bytes 491528 | tf_op jit(solution)/shard_map/ppermute | solution.py:585
  79.7 6.4 %all-to-all-start.1 = ((f32[256,4,128]{2,1,0:T(4,128)}), f32[256,4,128]{2,1,0:T(4,128)S(1)}, u32[]{:S(2)}, u32[]{:S(2)}) async-start(f32[256,4,128]{2,1,0:T(4,128)} %get-tuple-element.62), calls=%async_computation.1 | async-start | bytes 1048576 | tf_op jit(solution)/shard_map/all_to_all | solution.py:554
  89.6 8.7 %shard_map.93 = (f32[384,768]{1,0:T(8,128)S(1)}, f32[336,256]{1,0:T(8,128)S(1)}) custom-call(s32[2]{0:T(128)S(1)} %pad_add_fusion.pos_ref, f32[6,384,128]{2,1,0:T(8,128)S(1)} %copy-done.10, f32[2,624,128]{2,1,0:T(8,128)S(1)} %copy-done.16, bf16[48,1536]{1,0:T(8,128)(2,1)S(1)} %collective-permute-done.4.above_ref, bf16[48,1536]{1,0:T(8,128)(2,1)S(1)} %copy-done.20, ...), custom_call_target="tpu_custom_call" | custom-call | flops 10000000000 | bytes 9912328 | tf_op jit(solution)/shard_map/pallas_call | solution.py:45
  99.4 7.4 %all-to-all-done.1 = f32[256,4,128]{2,1,0:T(4,128)S(1)} async-done(((f32[256,4,128]{2,1,0:T(4,128)}), f32[256,4,128]{2,1,0:T(4,128)S(1)}, u32[]{:S(2)}, u32[]{:S(2)}) %all-to-all-start.1) | async-done | bytes 524320 | tf_op jit(solution)/shard_map/all_to_all | solution.py:554
  106.7 9.6 %shard_map.94 = (f32[384,768]{1,0:T(8,128)S(1)}, f32[256,1,128]{2,1,0:T(1,128)S(1)}, f32[8,128]{1,0:T(8,128)S(1)}) custom-call(s32[2]{0:T(128)S(1)} %pad_add_fusion.pos_ref, f32[1024,128]{1,0:T(8,128)S(1)} %bitcast.23, f32[1024,128]{1,0:T(8,128)S(1)} %bitcast.22, f32[384,768]{1,0:T(8,128)} %bitcast.16, f32[384,768]{1,0:T(8,128)} %get-tuple-element.63.u_ref, ...), custom_call_target="tpu_custom_call" | custom-call | flops 100000000 | bytes 8503304 | tf_op jit(solution)/shard_map/pallas_call | solution.py:45
  116.4 19.2 %all_to_all.15 = f32[256,1,128]{2,1,0:T(1,128)S(1)} all-to-all(f32[256,1,128]{2,1,0:T(1,128)S(1)} %get-tuple-element.69), channel_id=1, replica_groups=mesh['z'=8,'c'=2,'y'=4,'x1'=2,'x0'=2] {'c','x0','z','y','x1'}, dimensions={0} | all-to-all | bytes 262144 | tf_op jit(solution)/shard_map/all_to_all | solution.py:554
  135.6 1.8 %shard_map.95 = (f32[384,768]{1,0:T(8,128)}, f32[6,6]{1,0:T(8,128)}) custom-call(f32[256,128]{1,0:T(8,128)S(1)} %bitcast.27, f32[8,128]{1,0:T(8,128)S(1)} %get-tuple-element.70.totals_ref, f32[384,768]{1,0:T(8,128)S(1)} %bitcast.17, f32[384,768]{1,0:T(8,128)S(1)} %copy-done.5, f32[384,768]{1,0:T(8,128)S(1)} %get-tuple-element.71.v_ref), custom_call_target="tpu_custom_call" | custom-call | flops 1000000 | bytes 3674112 | tf_op jit(solution)/shard_map/pallas_call | solution.py:45
  (62 shorter events, 14.4 us)
Async XLA Ops:
  8.0 7.9 %copy-start.13 = (f32[2,624,128]{2,1,0:T(8,128)}, f32[2,624,128]{2,1,0:T(8,128)S(1)}, u32[]{:S(2)}) copy-start(f32[2,624,128]{2,1,0:T(8,128)S(1)} %get-tuple-element.41.tree_ref) | copy-start | bytes 1916932
  8.0 7.1 %collective-permute-start = (bf16[48,1536]{1,0:T(8,128)(2,1)S(1)}, bf16[48,1536]{1,0:T(8,128)(2,1)S(1)}, u32[]{:S(2)}, u32[]{:S(2)}) collective-permute-start(bf16[48,1536]{1,0:T(8,128)(2,1)S(1)} %get-tuple-element.42), channel_id=1, source_target_pairs={{0,16},{16,32},{32,48},{48,64},{64,80},{80,96},{96,112},{112,128},... | collective-permute-start | bytes 442376 | tf_op jit(solution)/shard_map/ppermute | solution.py:577
  11.1 4.9 %collective-permute-start.1 = (bf16[48,1536]{1,0:T(8,128)(2,1)S(1)}, bf16[48,1536]{1,0:T(8,128)(2,1)S(1)}, u32[]{:S(2)}, u32[]{:S(2)}) collective-permute-start(bf16[48,1536]{1,0:T(8,128)(2,1)S(1)} %get-tuple-element.43), channel_id=1, source_target_pairs={{0,240},{16,0},{32,16},{48,32},{64,48},{80,64},{96,80},{112,96},{1... | collective-permute-start | bytes 442376 | tf_op jit(solution)/shard_map/ppermute | solution.py:578
  13.9 1.2 copy-start.6
  17.3 22.0 %collective-permute-start.2 = (bf16[80,1024]{1,0:T(8,128)(2,1)}, bf16[80,1024]{1,0:T(8,128)(2,1)S(1)}, u32[]{:S(2)}, u32[]{:S(2)}) collective-permute-start(bf16[80,1024]{1,0:T(8,128)(2,1)} %get-tuple-element.47), channel_id=1, source_target_pairs={{0,1},{1,2},{2,3},{3,4},{4,5},{5,6},{6,7},{7,8},{8,9},{9,10},{10,1... | collective-permute-start | bytes 491528 | tf_op jit(solution)/shard_map/ppermute | solution.py:586
  18.5 20.8 %collective-permute-start.3 = (bf16[80,1024]{1,0:T(8,128)(2,1)S(1)}, bf16[80,1024]{1,0:T(8,128)(2,1)S(1)}, u32[]{:S(2)}, u32[]{:S(2)}) collective-permute-start(bf16[80,1024]{1,0:T(8,128)(2,1)S(1)} %get-tuple-element.48), channel_id=1, source_target_pairs={{0,15},{1,0},{2,1},{3,2},{4,3},{5,4},{6,5},{7,6},{8,7},{9,8},{10,9... | collective-permute-start | bytes 491528 | tf_op jit(solution)/shard_map/ppermute | solution.py:585
  22.2 32.4 %all-to-all-start = ((f32[256,4,128]{2,1,0:T(4,128)}), f32[256,4,128]{2,1,0:T(4,128)S(1)}, u32[]{:S(2)}, u32[]{:S(2)}) async-start(f32[256,4,128]{2,1,0:T(4,128)} %get-tuple-element.46), calls=%async_computation | async-start | bytes 1048576 | tf_op jit(solution)/shard_map/all_to_all | solution.py:554
  33.9 6.0 %copy-start.14 = (f32[2,624,128]{2,1,0:T(8,128)S(1)}, f32[2,624,128]{2,1,0:T(8,128)}, u32[]{:S(2)}) copy-start(f32[2,624,128]{2,1,0:T(8,128)} %copy-done.13) | copy-start | bytes 1916932
  36.9 1.2 copy-start.1
  39.3 15.3 %copy-start.4 = (f32[5,4,64,64]{3,2,1,0:T(8,128)S(1)}, f32[5,4,64,64]{3,2,1,0:T(8,128)}, u32[]{:S(2)}) copy-start(f32[5,4,64,64]{3,2,1,0:T(8,128)} %param.12) | copy-start | bytes 983044
  39.3 15.3 %copy-start.12 = (bf16[768,64]{0,1:T(8,128)(2,1)S(1)}, bf16[768,64]{0,1:T(8,128)(2,1)}, u32[]{:S(2)}) copy-start(bf16[768,64]{0,1:T(8,128)(2,1)} %param.11) | copy-start | bytes 294916
  39.3 15.3 %copy-start.18 = (f32[8,8,256]{2,1,0:T(8,128)S(1)}, f32[8,8,256]{2,1,0:T(8,128)}, u32[]{:S(2)}) copy-start(f32[8,8,256]{2,1,0:T(8,128)} %param.8) | copy-start | bytes 196612
  39.3 15.3 %copy-start.22 = (s32[8,8]{1,0:T(8,128)S(1)}, s32[8,8]{1,0:T(8,128)}, u32[]{:S(2)}) copy-start(s32[8,8]{1,0:T(8,128)} %occupied_ref.3) | copy-start | bytes 772
  65.8 9.1 %copy-start.15 = (f32[2,624,128]{2,1,0:T(8,128)}, f32[2,624,128]{2,1,0:T(8,128)S(1)}, u32[]{:S(2)}) copy-start(f32[2,624,128]{2,1,0:T(8,128)S(1)} %get-tuple-element.57.tree_ref) | copy-start | bytes 1916932
  65.8 3.6 %collective-permute-start.4 = (bf16[48,1536]{1,0:T(8,128)(2,1)S(1)}, bf16[48,1536]{1,0:T(8,128)(2,1)S(1)}, u32[]{:S(2)}, u32[]{:S(2)}) collective-permute-start(bf16[48,1536]{1,0:T(8,128)(2,1)S(1)} %get-tuple-element.58), channel_id=1, source_target_pairs={{0,16},{16,32},{32,48},{48,64},{64,80},{80,96},{96,112},{112,128},... | collective-permute-start | bytes 442376 | tf_op jit(solution)/shard_map/ppermute | solution.py:577
  67.3 4.8 %collective-permute-start.5 = (bf16[48,1536]{1,0:T(8,128)(2,1)S(1)}, bf16[48,1536]{1,0:T(8,128)(2,1)S(1)}, u32[]{:S(2)}, u32[]{:S(2)}) collective-permute-start(bf16[48,1536]{1,0:T(8,128)(2,1)S(1)} %get-tuple-element.59), channel_id=1, source_target_pairs={{0,240},{16,0},{32,16},{48,32},{64,48},{80,64},{96,80},{112,96},{1... | collective-permute-start | bytes 442376 | tf_op jit(solution)/shard_map/ppermute | solution.py:578
  72.1 7.6 %copy-start.19 = (bf16[48,1536]{1,0:T(8,128)(2,1)}, bf16[48,1536]{1,0:T(8,128)(2,1)S(1)}, u32[]{:S(2)}) copy-start(bf16[48,1536]{1,0:T(8,128)(2,1)S(1)} %collective-permute-done.5.below_ref) | copy-start | bytes 442372
  72.1 1.3 copy-start.9
  73.4 13.3 %copy-start.10 = (f32[6,384,128]{2,1,0:T(8,128)S(1)}, f32[6,384,128]{2,1,0:T(8,128)}, u32[]{:S(2)}) copy-start(f32[6,384,128]{2,1,0:T(8,128)} %get-tuple-element.56.src_ref) | copy-start | bytes 3538948
  74.9 11.2 %collective-permute-start.6 = (bf16[80,1024]{1,0:T(8,128)(2,1)}, bf16[80,1024]{1,0:T(8,128)(2,1)S(1)}, u32[]{:S(2)}, u32[]{:S(2)}) collective-permute-start(bf16[80,1024]{1,0:T(8,128)(2,1)} %get-tuple-element.64), channel_id=1, source_target_pairs={{0,1},{1,2},{2,3},{3,4},{4,5},{5,6},{6,7},{7,8},{8,9},{9,10},{10,1... | collective-permute-start | bytes 491528 | tf_op jit(solution)/shard_map/ppermute | solution.py:586
  75.2 11.6 %collective-permute-start.7 = (bf16[80,1024]{1,0:T(8,128)(2,1)}, bf16[80,1024]{1,0:T(8,128)(2,1)}, u32[]{:S(2)}, u32[]{:S(2)}) collective-permute-start(bf16[80,1024]{1,0:T(8,128)(2,1)} %get-tuple-element.65), channel_id=1, source_target_pairs={{0,15},{1,0},{2,1},{3,2},{4,3},{5,4},{6,5},{7,6},{8,7},{9,8},{10,9... | collective-permute-start | bytes 491528 | tf_op jit(solution)/shard_map/ppermute | solution.py:585
  79.7 27.1 %all-to-all-start.1 = ((f32[256,4,128]{2,1,0:T(4,128)}), f32[256,4,128]{2,1,0:T(4,128)S(1)}, u32[]{:S(2)}, u32[]{:S(2)}) async-start(f32[256,4,128]{2,1,0:T(4,128)} %get-tuple-element.62), calls=%async_computation.1 | async-start | bytes 1048576 | tf_op jit(solution)/shard_map/all_to_all | solution.py:554
  106.7 28.9 %copy-start = (f32[8,8,6,3,256]{4,1,3,2,0:T(8,128)S(1)}, f32[8,8,6,3,256]{4,1,3,2,0:T(8,128)}, u32[]{:S(2)}) copy-start(f32[8,8,6,3,256]{4,1,3,2,0:T(8,128)} %param.7) | copy-start | bytes 3538948
  106.7 28.9 %copy-start.5 = (f32[384,768]{1,0:T(8,128)S(1)}, f32[384,768]{1,0:T(8,128)}, u32[]{:S(2)}) copy-start(f32[384,768]{1,0:T(8,128)} %get-tuple-element.63.u_ref) | copy-start | bytes 3538948
  (13 other events, 11.9 us)

commit v2 on v1

--- a/solution.py
+++ b/solution.py
@@ -237,9 +237,15 @@
 
 
 def near_and_low(
-    pos_ref, src_ref, tree_ref, above_ref, below_ref, left_ref, right_ref, near_ref, inner_ref,
-    near_out, inner_out, wide, moved, edge, placed, n0, n1, n2, turned,
+    pos_ref, src_ref, tree_ref, above_ref, below_ref, left_ref, right_ref, near_hbm, inner_ref,
+    near_out, inner_out, near_ref, arrived, wide, moved, edge, placed, n0, n1, n2, turned,
 ):
+    copies = [
+        pltpu.make_async_copy(near_hbm.at[n], near_ref.at[n], arrived.at[n]) for n in range(5)
+    ]
+    for n in (2, 0, 3, 1, 4):
+        copies[n].start()
+    waited = set()
     gx, gy = pos_ref[0], pos_ref[1]
     up = (gx > 0).astype(F32)
     down = (gx < 15).astype(F32)
@@ -267,11 +273,15 @@
                 moved[t, pl.ds(7, 60, stride=8), :] = edge[0:60, lanes]
             placed[:, lanes] = moved[t].astype(BF16)
         for a in (-1, 0, 1):
+            slot = NEAR_SLOT[(a, b) if (a, b) in NEAR_SLOT else (-a, -b)]
+            if slot not in waited:
+                waited.add(slot)
+                copies[slot].wait()
             lhs = placed[48 * (1 + a) : 48 * (1 + a) + 384, :]
             if (a, b) in NEAR_SLOT:
-                part = dot(lhs, near_ref[NEAR_SLOT[a, b]])
+                part = dot(lhs, near_ref[slot])
             else:
-                part = dot_t(lhs, near_ref[NEAR_SLOT[-a, -b]])
+                part = dot_t(lhs, near_ref[slot])
             if first:
                 near_out[...] = part
                 first = False
@@ -588,8 +598,9 @@
         parts = call(
             near_and_low,
             [shape((384, 768), F32), shape((336, 256), F32)],
-            [SMEM] + [VMEM] * 8,
+            [SMEM] + [VMEM] * 6 + [pl.BlockSpec(memory_space=pl.ANY), VMEM],
             [
+                pltpu.VMEM((5, 768, 768), BF16), pltpu.SemaphoreType.DMA((5,)),
                 pltpu.VMEM((6, 480, 128), F32), pltpu.VMEM((6, 480, 128), F32), pltpu.VMEM((80, 768), F32),
                 pltpu.VMEM((480, 768), BF16), pltpu.VMEM((2, 288, 128), F32), pltpu.VMEM((2, 192, 128), F32),
                 pltpu.VMEM((2, 144, 128), F32), pltpu.VMEM((288, 256), F32),

time: 138 us -> 140 us (1.014)
  waiting for transfers between devices: 17 us -> 14.7 us
  Pallas kernels: 52.1 us -> 54.4 us
    all_to_all x2, waiting for transfers between devices: 11.4 us -> 9.13 us  [to_everyone(): return lax.all_to_all(blocks, CLASS_ORDER, 0, 0, tiled=True)]
    pallas_call x10, Pallas kernels: 52.1 us -> 54.4 us  [call(): pl.pallas_call(kernel, out_shape=outs, in_specs=specs, out_specs=jax.tree...]
  transfers between devices with their start and end apart: 10 -> 10, of which waited for: 5 -> 5; matrix products, arithmetic and copies ran while one was open for 0% -> 0% of each run, Pallas kernels for 17% -> 18%
where the time goes in v2:
time: 140 us
  Pallas kernels  54.4 us (39%)
  starting transfers between devices  33.7 us (24%)
  blocking collectives  20.4 us (15%)
  local copies, waits for them, and re-layouts  15.5 us (11%)
  waiting for transfers between devices  14.7 us (10%)
    pallas_call x10, Pallas kernels, call(): pl.pallas_call(kernel, out_shape=outs, in_specs=specs, out_specs=jax.tree...  54.4 us
    all_to_all x1, blocking collectives, to_everyone(): return lax.all_to_all(blocks, CLASS_ORDER, 0, 0, tiled=True)  20.4 us
    all_to_all x2, starting transfers between devices, to_everyone(): return lax.all_to_all(blocks, CLASS_ORDER, 0, 0, tiled=True)  19.2 us
    unnamed x54, local copies, waits for them, and re-layouts  15.5 us
    all_to_all x2, waiting for transfers between devices, to_everyone(): return lax.all_to_all(blocks, CLASS_ORDER, 0, 0, tiled=True)  9.13 us
    ppermute x2, starting transfers between devices, exchange(): right = lax.ppermute(to_left, GY, turn(16, -1))  8.21 us
    ppermute x2, starting transfers between devices, exchange(): above = lax.ppermute(up, GX, turn(16, 1))  4.55 us
    ppermute x2, waiting for transfers between devices, exchange(): below = lax.ppermute(down, GX, turn(16, -1))  3.49 us
  transfers between devices with their start and end apart: 10, of which 5 were waited for; matrix products, arithmetic and copies ran while one was open for 0% of the time, Pallas kernels for 18%

profile of v2, /device:TPU:1, one launch (start us, length us, event | category | flops | bytes accessed | tf_op | source)
XLA Modules:
  0.0 139.6 jit_solution(119570253941028892)
XLA Ops:
  4.1 3.9 %shard_map.86 = (f32[6,384,128]{2,1,0:T(8,128)S(1)}, bf16[48,1536]{1,0:T(8,128)(2,1)S(1)}, bf16[48,1536]{1,0:T(8,128)(2,1)S(1)}, f32[256,4,128]{2,1,0:T(4,128)}, f32[2,624,128]{2,1,0:T(8,128)S(1)}) custom-call(f32[384,768]{1,0:T(8,128)} %bitcast.14, f32[64,256]{1,0:T(8,128)S(1)} %bitcast.28, s32[8,8]{1,0:T(8,128)S(1)} %copy-done.21, ...), custom_call_target="tpu_custom_call" | custom-call | flops 100000000 | bytes 1671424 | tf_op jit(solution)/shard_map/pallas_call | solution.py:45
  8.0 3.0 %collective-permute-start = (bf16[48,1536]{1,0:T(8,128)(2,1)S(1)}, bf16[48,1536]{1,0:T(8,128)(2,1)S(1)}, u32[]{:S(2)}, u32[]{:S(2)}) collective-permute-start(bf16[48,1536]{1,0:T(8,128)(2,1)S(1)} %get-tuple-element.42), channel_id=1, source_target_pairs={{0,16},{16,32},{32,48},{48,64},{64,80},{80,96},{96,112},{112,128},... | collective-permute-start | bytes 442376 | tf_op jit(solution)/shard_map/ppermute | solution.py:587
  11.3 2.6 %shard_map.87.inner_ref = bf16[3,4,256,256]{3,2,1,0:T(8,128)(2,1)S(1)} custom-call(f32[6,20,64,64]{3,2,1,0:T(8,128)} %coupling_ref.3), custom_call_target="tpu_custom_call" | custom-call | flops 100000000 | bytes 1966080 | tf_op jit(solution)/shard_map/pallas_call | solution.py:45
  13.9 1.2 copy-done.6
  15.9 1.4 shard_map.88
  17.3 1.2 collective-permute-start.2
  18.5 3.7 %collective-permute-start.3 = (bf16[80,1024]{1,0:T(8,128)(2,1)S(1)}, bf16[80,1024]{1,0:T(8,128)(2,1)S(1)}, u32[]{:S(2)}, u32[]{:S(2)}) collective-permute-start(bf16[80,1024]{1,0:T(8,128)(2,1)S(1)} %get-tuple-element.48), channel_id=1, source_target_pairs={{0,15},{1,0},{2,1},{3,2},{4,3},{5,4},{6,5},{7,6},{8,7},{9,8},{10,9... | collective-permute-start | bytes 491528 | tf_op jit(solution)/shard_map/ppermute | solution.py:595
  22.2 11.7 %all-to-all-start = ((f32[256,4,128]{2,1,0:T(4,128)}), f32[256,4,128]{2,1,0:T(4,128)S(1)}, u32[]{:S(2)}, u32[]{:S(2)}) async-start(f32[256,4,128]{2,1,0:T(4,128)} %get-tuple-element.46), calls=%async_computation | async-start | bytes 1048576 | tf_op jit(solution)/shard_map/all_to_all | solution.py:564
  33.9 3.0 %shard_map.90 = (bf16[3,4,256,256]{3,2,1,0:T(8,128)(2,1)S(1)}, bf16[3,4,256,256]{3,2,1,0:T(8,128)(2,1)S(1)}) custom-call(f32[6,20,64,64]{3,2,1,0:T(8,128)} %coupling_ref.3), custom_call_target="tpu_custom_call" | custom-call | flops 100000000 | bytes 1966080 | tf_op jit(solution)/shard_map/pallas_call | solution.py:45
  40.9 9.8 %shard_map.89 = (f32[384,768]{1,0:T(8,128)S(1)}, f32[336,256]{1,0:T(8,128)S(1)}) custom-call(s32[2]{0:T(128)S(1)} %pad_add_fusion.pos_ref, f32[6,384,128]{2,1,0:T(8,128)S(1)} %get-tuple-element.40.src_ref, f32[2,624,128]{2,1,0:T(8,128)S(1)} %copy-done.14, bf16[48,1536]{1,0:T(8,128)(2,1)S(1)} %collective-permute-done.above_ref, ...), custom_call_target="tpu_custom_call" | custom-call | flops 10000000000 | bytes 9912328 | tf_op jit(solution)/shard_map/pallas_call | solution.py:45
  51.7 2.9 %all-to-all-done = f32[256,4,128]{2,1,0:T(4,128)S(1)} async-done(((f32[256,4,128]{2,1,0:T(4,128)}), f32[256,4,128]{2,1,0:T(4,128)S(1)}, u32[]{:S(2)}, u32[]{:S(2)}) %all-to-all-start) | async-done | bytes 524320 | tf_op jit(solution)/shard_map/all_to_all | solution.py:564
  54.6 11.2 %shard_map.91 = (f32[384,768]{1,0:T(8,128)}, f32[6,384,128]{2,1,0:T(8,128)}, bf16[48,1536]{1,0:T(8,128)(2,1)S(1)}, bf16[48,1536]{1,0:T(8,128)(2,1)S(1)}, f32[256...) custom-call(s32[2]{0:T(128)S(1)} %pad_add_fusion.pos_ref, f32[1024,128]{1,0:T(8,128)S(1)} %bitcast.21, f32[384,768]{1,0:T(8,128)} %bitcast.15, ...), custom_call_target="tpu_custom_call" | custom-call | flops 100000000 | bytes 6865160 | tf_op jit(solution)/shard_map/pallas_call | solution.py:45
  65.8 1.5 %collective-permute-start.4 = (bf16[48,1536]{1,0:T(8,128)(2,1)S(1)}, bf16[48,1536]{1,0:T(8,128)(2,1)S(1)}, u32[]{:S(2)}, u32[]{:S(2)}) collective-permute-start(bf16[48,1536]{1,0:T(8,128)(2,1)S(1)} %get-tuple-element.58), channel_id=1, source_target_pairs={{0,16},{16,32},{32,48},{48,64},{64,80},{80,96},{96,112},{112,128},... | collective-permute-start | bytes 442376 | tf_op jit(solution)/shard_map/ppermute | solution.py:587
  67.3 2.1 %collective-permute-done.4.above_ref = bf16[48,1536]{1,0:T(8,128)(2,1)S(1)} collective-permute-done((bf16[48,1536]{1,0:T(8,128)(2,1)S(1)}, bf16[48,1536]{1,0:T(8,128)(2,1)S(1)}, u32[]{:S(2)}, u32[]{:S(2)}) %collective-permute-start.4) | collective-permute-done | bytes 147488 | tf_op jit(solution)/shard_map/ppermute | solution.py:587
  69.4 2.7 %collective-permute-done.5.below_ref = bf16[48,1536]{1,0:T(8,128)(2,1)S(1)} collective-permute-done((bf16[48,1536]{1,0:T(8,128)(2,1)S(1)}, bf16[48,1536]{1,0:T(8,128)(2,1)S(1)}, u32[]{:S(2)}, u32[]{:S(2)}) %collective-permute-start.5) | collective-permute-done | bytes 147488 | tf_op jit(solution)/shard_map/ppermute | solution.py:588
  72.1 1.3 copy-done.9
  73.4 1.4 %shard_map.92 = (bf16[80,1024]{1,0:T(8,128)(2,1)}, bf16[80,1024]{1,0:T(8,128)(2,1)}) custom-call(s32[2]{0:T(128)S(1)} %pad_add_fusion.pos_ref, f32[6,384,128]{2,1,0:T(8,128)S(1)} %copy-done.9, f32[2,624,128]{2,1,0:T(8,128)S(1)} %get-tuple-element.57.tree_ref, bf16[48,1536]{1,0:T(8,128)(2,1)S(1)} %collective-permute-done.4.above_ref, ...), custom_call_target="tpu_custom_call" | custom-call | flops 1000000 | bytes 2113544 | tf_op jit(solution)/shard_map/pallas_call | solution.py:45
  75.2 4.5 %collective-permute-start.7 = (bf16[80,1024]{1,0:T(8,128)(2,1)}, bf16[80,1024]{1,0:T(8,128)(2,1)}, u32[]{:S(2)}, u32[]{:S(2)}) collective-permute-start(bf16[80,1024]{1,0:T(8,128)(2,1)} %get-tuple-element.65), channel_id=1, source_target_pairs={{0,15},{1,0},{2,1},{3,2},{4,3},{5,4},{6,5},{7,6},{8,7},{9,8},{10,9... | collective-permute-start | bytes 491528 | tf_op jit(solution)/shard_map/ppermute | solution.py:595
  79.7 7.5 %all-to-all-start.1 = ((f32[256,4,128]{2,1,0:T(4,128)}), f32[256,4,128]{2,1,0:T(4,128)S(1)}, u32[]{:S(2)}, u32[]{:S(2)}) async-start(f32[256,4,128]{2,1,0:T(4,128)} %get-tuple-element.62), calls=%async_computation.1 | async-start | bytes 1048576 | tf_op jit(solution)/shard_map/all_to_all | solution.py:564
  90.8 9.9 %shard_map.93 = (f32[384,768]{1,0:T(8,128)S(1)}, f32[336,256]{1,0:T(8,128)S(1)}) custom-call(s32[2]{0:T(128)S(1)} %pad_add_fusion.pos_ref, f32[6,384,128]{2,1,0:T(8,128)S(1)} %copy-done.10, f32[2,624,128]{2,1,0:T(8,128)S(1)} %copy-done.16, bf16[48,1536]{1,0:T(8,128)(2,1)S(1)} %collective-permute-done.4.above_ref, bf16[48,1536]{1,0:T(8,128)(2,1)S(1)} %copy-done.20, ...), custom_call_target="tpu_custom_call" | custom-call | flops 10000000000 | bytes 9912328 | tf_op jit(solution)/shard_map/pallas_call | solution.py:45
  101.6 6.2 %all-to-all-done.1 = f32[256,4,128]{2,1,0:T(4,128)S(1)} async-done(((f32[256,4,128]{2,1,0:T(4,128)}), f32[256,4,128]{2,1,0:T(4,128)S(1)}, u32[]{:S(2)}, u32[]{:S(2)}) %all-to-all-start.1) | async-done | bytes 524320 | tf_op jit(solution)/shard_map/all_to_all | solution.py:564
  107.9 9.6 %shard_map.94 = (f32[384,768]{1,0:T(8,128)S(1)}, f32[256,1,128]{2,1,0:T(1,128)S(1)}, f32[8,128]{1,0:T(8,128)S(1)}) custom-call(s32[2]{0:T(128)S(1)} %pad_add_fusion.pos_ref, f32[1024,128]{1,0:T(8,128)S(1)} %bitcast.23, f32[1024,128]{1,0:T(8,128)S(1)} %bitcast.22, f32[384,768]{1,0:T(8,128)} %bitcast.16, f32[384,768]{1,0:T(8,128)} %get-tuple-element.63.u_ref, ...), custom_call_target="tpu_custom_call" | custom-call | flops 100000000 | bytes 8503304 | tf_op jit(solution)/shard_map/pallas_call | solution.py:45
  117.5 20.4 %all_to_all.15 = f32[256,1,128]{2,1,0:T(1,128)S(1)} all-to-all(f32[256,1,128]{2,1,0:T(1,128)S(1)} %get-tuple-element.69), channel_id=1, replica_groups=mesh['z'=8,'c'=2,'y'=4,'x1'=2,'x0'=2] {'c','x0','z','y','x1'}, dimensions={0} | all-to-all | bytes 262144 | tf_op jit(solution)/shard_map/all_to_all | solution.py:564
  137.9 1.8 %shard_map.95 = (f32[384,768]{1,0:T(8,128)}, f32[6,6]{1,0:T(8,128)}) custom-call(f32[256,128]{1,0:T(8,128)S(1)} %bitcast.27, f32[8,128]{1,0:T(8,128)S(1)} %get-tuple-element.70.totals_ref, f32[384,768]{1,0:T(8,128)S(1)} %bitcast.17, f32[384,768]{1,0:T(8,128)S(1)} %copy-done.5, f32[384,768]{1,0:T(8,128)S(1)} %get-tuple-element.71.v_ref), custom_call_target="tpu_custom_call" | custom-call | flops 1000000 | bytes 3674112 | tf_op jit(solution)/shard_map/pallas_call | solution.py:45
  (62 shorter events, 14.4 us)
Async XLA Ops:
  8.0 7.9 %copy-start.13 = (f32[2,624,128]{2,1,0:T(8,128)}, f32[2,624,128]{2,1,0:T(8,128)S(1)}, u32[]{:S(2)}) copy-start(f32[2,624,128]{2,1,0:T(8,128)S(1)} %get-tuple-element.41.tree_ref) | copy-start | bytes 1916932
  8.0 7.1 %collective-permute-start = (bf16[48,1536]{1,0:T(8,128)(2,1)S(1)}, bf16[48,1536]{1,0:T(8,128)(2,1)S(1)}, u32[]{:S(2)}, u32[]{:S(2)}) collective-permute-start(bf16[48,1536]{1,0:T(8,128)(2,1)S(1)} %get-tuple-element.42), channel_id=1, source_target_pairs={{0,16},{16,32},{32,48},{48,64},{64,80},{80,96},{96,112},{112,128},... | collective-permute-start | bytes 442376 | tf_op jit(solution)/shard_map/ppermute | solution.py:587
  11.1 4.9 %collective-permute-start.1 = (bf16[48,1536]{1,0:T(8,128)(2,1)S(1)}, bf16[48,1536]{1,0:T(8,128)(2,1)S(1)}, u32[]{:S(2)}, u32[]{:S(2)}) collective-permute-start(bf16[48,1536]{1,0:T(8,128)(2,1)S(1)} %get-tuple-element.43), channel_id=1, source_target_pairs={{0,240},{16,0},{32,16},{48,32},{64,48},{80,64},{96,80},{112,96},{1... | collective-permute-start | bytes 442376 | tf_op jit(solution)/shard_map/ppermute | solution.py:588
  13.9 1.2 copy-start.6
  17.3 22.0 %collective-permute-start.2 = (bf16[80,1024]{1,0:T(8,128)(2,1)}, bf16[80,1024]{1,0:T(8,128)(2,1)S(1)}, u32[]{:S(2)}, u32[]{:S(2)}) collective-permute-start(bf16[80,1024]{1,0:T(8,128)(2,1)} %get-tuple-element.47), channel_id=1, source_target_pairs={{0,1},{1,2},{2,3},{3,4},{4,5},{5,6},{6,7},{7,8},{8,9},{9,10},{10,1... | collective-permute-start | bytes 491528 | tf_op jit(solution)/shard_map/ppermute | solution.py:596
  18.5 20.8 %collective-permute-start.3 = (bf16[80,1024]{1,0:T(8,128)(2,1)S(1)}, bf16[80,1024]{1,0:T(8,128)(2,1)S(1)}, u32[]{:S(2)}, u32[]{:S(2)}) collective-permute-start(bf16[80,1024]{1,0:T(8,128)(2,1)S(1)} %get-tuple-element.48), channel_id=1, source_target_pairs={{0,15},{1,0},{2,1},{3,2},{4,3},{5,4},{6,5},{7,6},{8,7},{9,8},{10,9... | collective-permute-start | bytes 491528 | tf_op jit(solution)/shard_map/ppermute | solution.py:595
  22.2 32.4 %all-to-all-start = ((f32[256,4,128]{2,1,0:T(4,128)}), f32[256,4,128]{2,1,0:T(4,128)S(1)}, u32[]{:S(2)}, u32[]{:S(2)}) async-start(f32[256,4,128]{2,1,0:T(4,128)} %get-tuple-element.46), calls=%async_computation | async-start | bytes 1048576 | tf_op jit(solution)/shard_map/all_to_all | solution.py:564
  33.9 6.0 %copy-start.14 = (f32[2,624,128]{2,1,0:T(8,128)S(1)}, f32[2,624,128]{2,1,0:T(8,128)}, u32[]{:S(2)}) copy-start(f32[2,624,128]{2,1,0:T(8,128)} %copy-done.13) | copy-start | bytes 1916932
  36.9 1.2 copy-start.1
  39.3 15.3 %copy-start.4 = (f32[5,4,64,64]{3,2,1,0:T(8,128)S(1)}, f32[5,4,64,64]{3,2,1,0:T(8,128)}, u32[]{:S(2)}) copy-start(f32[5,4,64,64]{3,2,1,0:T(8,128)} %param.12) | copy-start | bytes 983044
  39.3 15.3 %copy-start.12 = (bf16[768,64]{0,1:T(8,128)(2,1)S(1)}, bf16[768,64]{0,1:T(8,128)(2,1)}, u32[]{:S(2)}) copy-start(bf16[768,64]{0,1:T(8,128)(2,1)} %param.11) | copy-start | bytes 294916
  39.3 15.3 %copy-start.18 = (f32[8,8,256]{2,1,0:T(8,128)S(1)}, f32[8,8,256]{2,1,0:T(8,128)}, u32[]{:S(2)}) copy-start(f32[8,8,256]{2,1,0:T(8,128)} %param.8) | copy-start | bytes 196612
  39.3 15.3 %copy-start.22 = (s32[8,8]{1,0:T(8,128)S(1)}, s32[8,8]{1,0:T(8,128)}, u32[]{:S(2)}) copy-start(s32[8,8]{1,0:T(8,128)} %occupied_ref.3) | copy-start | bytes 772
  65.8 9.1 %copy-start.15 = (f32[2,624,128]{2,1,0:T(8,128)}, f32[2,624,128]{2,1,0:T(8,128)S(1)}, u32[]{:S(2)}) copy-start(f32[2,624,128]{2,1,0:T(8,128)S(1)} %get-tuple-element.57.tree_ref) | copy-start | bytes 1916932
  65.8 3.6 %collective-permute-start.4 = (bf16[48,1536]{1,0:T(8,128)(2,1)S(1)}, bf16[48,1536]{1,0:T(8,128)(2,1)S(1)}, u32[]{:S(2)}, u32[]{:S(2)}) collective-permute-start(bf16[48,1536]{1,0:T(8,128)(2,1)S(1)} %get-tuple-element.58), channel_id=1, source_target_pairs={{0,16},{16,32},{32,48},{48,64},{64,80},{80,96},{96,112},{112,128},... | collective-permute-start | bytes 442376 | tf_op jit(solution)/shard_map/ppermute | solution.py:587
  67.3 4.8 %collective-permute-start.5 = (bf16[48,1536]{1,0:T(8,128)(2,1)S(1)}, bf16[48,1536]{1,0:T(8,128)(2,1)S(1)}, u32[]{:S(2)}, u32[]{:S(2)}) collective-permute-start(bf16[48,1536]{1,0:T(8,128)(2,1)S(1)} %get-tuple-element.59), channel_id=1, source_target_pairs={{0,240},{16,0},{32,16},{48,32},{64,48},{80,64},{96,80},{112,96},{1... | collective-permute-start | bytes 442376 | tf_op jit(solution)/shard_map/ppermute | solution.py:588
  72.1 7.6 %copy-start.19 = (bf16[48,1536]{1,0:T(8,128)(2,1)}, bf16[48,1536]{1,0:T(8,128)(2,1)S(1)}, u32[]{:S(2)}) copy-start(bf16[48,1536]{1,0:T(8,128)(2,1)S(1)} %collective-permute-done.5.below_ref) | copy-start | bytes 442372
  72.1 1.3 copy-start.9
  73.4 14.4 %copy-start.10 = (f32[6,384,128]{2,1,0:T(8,128)S(1)}, f32[6,384,128]{2,1,0:T(8,128)}, u32[]{:S(2)}) copy-start(f32[6,384,128]{2,1,0:T(8,128)} %get-tuple-element.56.src_ref) | copy-start | bytes 3538948
  74.9 12.3 %collective-permute-start.6 = (bf16[80,1024]{1,0:T(8,128)(2,1)}, bf16[80,1024]{1,0:T(8,128)(2,1)S(1)}, u32[]{:S(2)}, u32[]{:S(2)}) collective-permute-start(bf16[80,1024]{1,0:T(8,128)(2,1)} %get-tuple-element.64), channel_id=1, source_target_pairs={{0,1},{1,2},{2,3},{3,4},{4,5},{5,6},{6,7},{7,8},{8,9},{9,10},{10,1... | collective-permute-start | bytes 491528 | tf_op jit(solution)/shard_map/ppermute | solution.py:596
  75.2 12.7 %collective-permute-start.7 = (bf16[80,1024]{1,0:T(8,128)(2,1)}, bf16[80,1024]{1,0:T(8,128)(2,1)}, u32[]{:S(2)}, u32[]{:S(2)}) collective-permute-start(bf16[80,1024]{1,0:T(8,128)(2,1)} %get-tuple-element.65), channel_id=1, source_target_pairs={{0,15},{1,0},{2,1},{3,2},{4,3},{5,4},{6,5},{7,6},{8,7},{9,8},{10,9... | collective-permute-start | bytes 491528 | tf_op jit(solution)/shard_map/ppermute | solution.py:595
  79.7 28.2 %all-to-all-start.1 = ((f32[256,4,128]{2,1,0:T(4,128)}), f32[256,4,128]{2,1,0:T(4,128)S(1)}, u32[]{:S(2)}, u32[]{:S(2)}) async-start(f32[256,4,128]{2,1,0:T(4,128)} %get-tuple-element.62), calls=%async_computation.1 | async-start | bytes 1048576 | tf_op jit(solution)/shard_map/all_to_all | solution.py:564
  107.8 30.0 %copy-start = (f32[8,8,6,3,256]{4,1,3,2,0:T(8,128)S(1)}, f32[8,8,6,3,256]{4,1,3,2,0:T(8,128)}, u32[]{:S(2)}) copy-start(f32[8,8,6,3,256]{4,1,3,2,0:T(8,128)} %param.7) | copy-start | bytes 3538948
  107.8 30.0 %copy-start.5 = (f32[384,768]{1,0:T(8,128)S(1)}, f32[384,768]{1,0:T(8,128)}, u32[]{:S(2)}) copy-start(f32[384,768]{1,0:T(8,128)} %get-tuple-element.63.u_ref) | copy-start | bytes 3538948
  (13 other events, 11.9 us)
